TPU v7x, 32 devices: a whole 2x2x4 slice. The times are simulated.
32 devices in a mesh: ap: 16 (over z, y, x), sc: 2 (over core).
Axes of the slice: x: 2, y: 2, z: 4, core: 2. Of those that a mesh axis runs over, the one named last changes fastest.
Arguments:
- covariances: float32 [512, 512], P('ap'), as said below
- clusters: int32 [512, 16], P('ap'), may hold values from 0 to 255, as said below
- cluster_valid: int32 [512, 16], P('ap'), may hold values 0 or 1
- pilots: int32 [512], P('ap'), may hold values from 0 to 15
- received_pilot: float32 [256, 16, 128], P('ap', 'sc'), may hold values from -9 to 9
- received_data: float32 [256, 16, 128], P('ap', 'sc'), may hold values from -18 to 18
Outputs:
- symbols_out: float32 [512, 16, 32], P('ap', 'sc')
- gain_out: float32 [512, 16], P('ap', 'sc')
Inputs may be any that keep to these rules, and one draw needn't show every extreme that they name: `clusters`: the 16 ids in one user's row differ and lie on 16 different indices of ap (ids l with l // 16 = index); within the 32 users of one aligned block (the users of one device), the slots whose ids lie on one index of ap number exactly 32 for every index. `covariances`: each row-major 4 x 4 complex matrix is Hermitian positive definite.
All inputs are finite; a program needn't handle non-finite values. No bound on the sum of `cluster_valid` on one device may be relied on, other than what follows from the above.
Results may differ from a plain program's by a relative error of at most 0.00011.
Values sent between devices are 32-bit elements; how exact they have to be, the bound alone decides.
A program may use at most 64 MiB of HBM per device.

v0:
```python
import functools

import jax
import jax.numpy as jnp
from jax import lax
from jax.experimental import pallas as pl
from jax.experimental.pallas import tpu as pltpu
from jax.sharding import PartitionSpec as P

F32 = jnp.float32
BF16 = jnp.bfloat16
MESH = pl.DeviceIdType.MESH
PAIRS = [(0, 1), (0, 2), (0, 3), (1, 2), (1, 3), (2, 3)]
ENTRIES = [(i, i) for i in range(4)] + PAIRS


def split(x, parts):
    out = []
    for _ in range(parts - 1):
        head = x.astype(BF16)
        out.append(head)
        x = x - head.astype(F32)
    out.append(x.astype(BF16))
    return out


def dot(a, b, rhs_transposed=False):
    dims = (((1,), (1,)), ((), ())) if rhs_transposed else (((1,), (0,)), ((), ()))
    return lax.dot_general(a, b, dims, preferred_element_type=F32)


def dot_split(a, b, parts, rhs_transposed=False):
    rows = a.shape[0]
    full = dot(jnp.concatenate(split(a, parts), 0), b, rhs_transposed)
    total = full[:rows]
    for p in range(1, parts):
        total = total + full[p * rows : (p + 1) * rows]
    return total


def get(h, i, j):
    if i == j:
        return h[i, i]
    if i < j:
        return h[i, j]
    re, im = h[j, i]
    return re, -im


def hermitian_inverse(h):
    h = dict(h)
    for k in range(4):
        inv = 1.0 / h[k, k][0]
        col = {i: get(h, i, k) for i in range(4) if i != k}
        scaled = {i: (c[0] * inv, c[1] * inv) for i, c in col.items()}
        new = {}
        for i, j in ENTRIES:
            if i == k and j == k:
                new[i, j] = (-inv, None)
            elif i == k:
                re, im = scaled[j]
                new[i, j] = (re, -im)
            elif j == k:
                new[i, j] = scaled[i]
            elif i == j:
                a, s = col[i], scaled[i]
                new[i, j] = (h[i, i][0] - (a[0] * s[0] + a[1] * s[1]), None)
            else:
                a, s = scaled[i], col[j]
                re = h[i, j][0] - (a[0] * s[0] + a[1] * s[1])
                im = h[i, j][1] - (a[1] * s[0] - a[0] * s[1])
                new[i, j] = (re, im)
        h = new
    return {k: (-v[0], None if v[1] is None else -v[1]) for k, v in h.items()}


def parts_of(h):
    out = [h[i, i][0] for i in range(4)]
    for p in PAIRS:
        out += list(h[p])
    return out


def from_parts(x):
    h = {(i, i): (x[i], None) for i in range(4)}
    for q, p in enumerate(PAIRS):
        h[p] = (x[4 + 2 * q], x[5 + 2 * q])
    return h


def add_products(acc, a, b):
    re, im = a[0] * b[0], None
    if a[1] is not None and b[1] is not None:
        re = re - a[1] * b[1]
    if b[1] is not None:
        im = a[0] * b[1]
    if a[1] is not None:
        im = a[1] * b[0] if im is None else im + a[1] * b[0]
    if acc is None:
        return re, im
    if im is None:
        im = acc[1]
    elif acc[1] is not None:
        im = acc[1] + im
    return acc[0] + re, im


def block_transpose(x):
    lane_block = lax.broadcasted_iota(jnp.int32, x[0].shape, 1) // 16
    x = list(x)
    for m in (1, 2, 4):
        upper = (lane_block & m) != 0
        new = list(x)
        for p in range(8):
            if p & m:
                continue
            q = p + m
            new[p] = jnp.where(upper, pltpu.roll(x[q], 16 * m, 1), x[p])
            new[q] = jnp.where(upper, x[q], pltpu.roll(x[p], 128 - 16 * m, 1))
        x = new
    return x


def lane_groups(x):
    lane_block = lax.broadcasted_iota(jnp.int32, x[0].shape, 1) // 32
    x = list(x)
    for m in (1, 2):
        upper = (lane_block & m) != 0
        new = list(x)
        for p in range(4):
            if p & m:
                continue
            q = p + m
            new[p] = jnp.where(upper, pltpu.roll(x[q], 32 * m, 1), x[p])
            new[q] = jnp.where(upper, x[q], pltpu.roll(x[p], 128 - 32 * m, 1))
        x = new
    return x


def kernel(
    n, cov_hbm, cl_hbm, valid_hbm, pilot_hbm, rp_hbm, rd_hbm, sym_ref, gain_ref,
    cov_ref, cl_ref, valid_ref, pilot_ref, rp_ref, rd_ref,
    send, recv, trans, pinv, obs, data, data_in, wide_data, out_w, in_w, back, home,
    load_sem, send_sem, recv_sem, data_send_sem, data_recv_sem,
    w_send_sem, w_recv_sem, back_send_sem, back_recv_sem,
):
    me = lax.axis_index("ap")
    core = lax.axis_index("sc")
    rows = n // 4
    sets = n // 16
    groups = 4 * sets
    q, z = lax.div(me, rows), lax.rem(me, rows)

    pairs = [
        (cl_hbm, cl_ref), (valid_hbm, valid_ref), (pilot_hbm, pilot_ref),
        (cov_hbm, cov_ref), (rp_hbm, rp_ref), (rd_hbm, rd_ref),
    ]
    loads = [pltpu.make_async_copy(a, b, load_sem.at[i]) for i, (a, b) in enumerate(pairs)]
    for load in loads:
        load.start()

    barrier = pltpu.get_barrier_semaphore()

    @pl.loop(1, n)
    def _(d):
        pl.semaphore_signal(barrier, inc=1, device_id=(lax.rem(me + d, n), core), device_id_type=MESH)

    lane = lax.broadcasted_iota(jnp.int32, (32, 1024), 1)
    spread = (lane // 32 == lax.broadcasted_iota(jnp.int32, (32, 1024), 0)).astype(F32).astype(BF16)
    lane32 = lax.broadcasted_iota(jnp.int32, (32, 512), 1)
    quarter = lax.broadcasted_iota(jnp.int32, (8, 128), 1) // 32
    for load in loads[:4]:
        load.wait()
    cl = cl_ref[...]
    code = jnp.where(
        valid_ref[...] > 0, (pilot_ref[...] * 16 + (cl & 15)).astype(F32) + 1.0, 0.0
    )
    small = jnp.concatenate([(cl >> 4).astype(F32), code], 0).T
    wide = dot(small.astype(BF16), spread)
    owner_w, code_w = wide[:, :512], wide[:, 512:]
    payload = jnp.where((lane32 & 31) == 16, code_w, cov_ref[...])
    for t in range(n):
        m = jnp.where(owner_w == float(t), payload, 0.0)
        s = m[:, 0:128] + m[:, 128:256] + (m[:, 256:384] + m[:, 384:512])
        s = s + pltpu.roll(s, 64, 1)
        s = s + pltpu.roll(s, 32, 1)
        packed = s[0:8]
        for j in range(1, 4):
            packed = jnp.where(quarter == j, s[8 * j : 8 * j + 8], packed)
        send[t] = packed

    pl.semaphore_wait(barrier, n - 1)

    def slot_copy(p, slot):
        return pltpu.make_async_remote_copy(
            src_ref=send.at[p], dst_ref=recv.at[slot],
            send_sem=send_sem.at[p], recv_sem=recv_sem.at[slot],
            device_id=(p, core), device_id_type=MESH,
        )

    def data_copy(p, slot):
        return pltpu.make_async_remote_copy(
            src_ref=data, dst_ref=data_in.at[slot],
            send_sem=data_send_sem.at[p], recv_sem=data_recv_sem.at[slot],
            device_id=(q * rows + p, core), device_id_type=MESH,
        )

    def w_copy(p, slot):
        return pltpu.make_async_remote_copy(
            src_ref=out_w.at[p], dst_ref=in_w.at[slot],
            send_sem=w_send_sem.at[p], recv_sem=w_recv_sem.at[slot],
            device_id=(q * rows + p, core), device_id_type=MESH,
        )

    def back_copy(p, slot):
        return pltpu.make_async_remote_copy(
            src_ref=back.at[p], dst_ref=home.at[slot],
            send_sem=back_send_sem.at[p], recv_sem=back_recv_sem.at[slot],
            device_id=(p * rows + z, core), device_id_type=MESH,
        )

    @pl.loop(1, n)
    def _(d):
        p = lax.rem(me + d, n)
        slot_copy(p, me).start()

    recv[me] = send[me]

    for load in loads[4:]:
        load.wait()
    turned = jnp.concatenate([rd_ref[:, f, :] for f in range(8)], 0).T.reshape(16, 8, 128)
    for f, tile in enumerate(block_transpose([turned[:, i, :] for i in range(8)])):
        data[:, f, :] = tile

    @pl.loop(1, rows)
    def _(d):
        data_copy(lax.rem(z + d, rows), z).start()

    turned = jnp.concatenate([rp_ref[:, f, :] for f in range(8)], 0).T
    for half in range(2):
        tiles = [turned[8 * (8 * half + t) : 8 * (8 * half + t) + 8] for t in range(8)]
        for f, tile in enumerate(block_transpose(tiles)):
            obs[f, :, 128 * half : 128 * half + 128] = tile
    observed = jnp.concatenate([obs[:, i, :] for i in range(8)], 0)
    observed = jnp.concatenate(split(observed, 3), 0)

    @pl.loop(1, n)
    def _(d):
        p = lax.rem(me + n - d, n)
        slot_copy(p, p).wait_recv()

    row32 = lax.broadcasted_iota(jnp.int32, (32, 128), 0)
    codes, matrices = [], []
    for e in range(sets):
        block = jnp.concatenate([recv[h * rows + 4 * e + l] for l in range(4) for h in range(4)], 0).T
        for j, tile in enumerate(lane_groups([block[32 * j : 32 * j + 32] for j in range(4)])):
            trans[e, j] = tile
            codes.append(tile[16:17])
            matrices.append(jnp.where(row32 == 16, 0.0, tile))
    codes = jnp.concatenate(codes, 1) - 1.0
    matrices = jnp.concatenate(matrices, 1)
    width = 128 * groups
    bins = lax.broadcasted_iota(jnp.int32, (256, width), 0).astype(F32)
    choose = jnp.where(bins == codes, 1.0, 0.0).astype(BF16)
    places = jnp.where(codes >= 0.0, codes - 16.0 * jnp.floor(codes * 0.0625), -1.0)
    ap_rows = (lax.broadcasted_iota(jnp.int32, (128, width), 0) & 15).astype(F32)
    pick = jnp.where(ap_rows == places, 1.0, 0.0).astype(BF16)

    psi = dot_split(matrices, choose, 3, True)
    at = lambda x, i, j: (x[4 * i + j : 4 * i + j + 1], x[16 + 4 * i + j : 17 + 4 * i + j])
    hermitian = {(i, i): (at(psi, i, i)[0] + 1.0, None) for i in range(4)}
    hermitian.update({p: at(psi, *p) for p in PAIRS})
    inverse = jnp.concatenate(parts_of(hermitian_inverse(hermitian)), 0)
    slot_inverse = dot_split(inverse, choose, 3)
    slot_obs = dot(observed, choose)
    slot_obs = slot_obs[0:64] + slot_obs[64:128] + slot_obs[128:192]

    estimates, outers = [], []
    for e in range(sets):
        for j in range(4):
            g = 4 * e + j
            pinv[j] = slot_inverse[:, 128 * g : 128 * g + 128]
        pi = from_parts([pinv[:, x, :] for x in range(16)])
        r = {(i, i): (trans[e, :, 5 * i, :], None) for i in range(4)}
        for i, k in PAIRS:
            r[i, k] = (trans[e, :, 4 * i + k, :], trans[e, :, 16 + 4 * i + k, :])
        w = {}
        for i in range(4):
            for k in range(4):
                acc = None
                for l in range(4):
                    acc = add_products(acc, get(r, i, l), get(pi, l, k))
                w[i, k] = acc
        err = {}
        for i, k in ENTRIES:
            acc = None
            for l in range(4):
                acc = add_products(acc, w[i, l], get(r, l, k))
            re = r[i, k][0] - acc[0]
            err[i, k] = (re, None) if i == k else (re, r[i, k][1] - acc[1])
        for j in range(4):
            g = 4 * e + j
            cols = slice(128 * g, 128 * g + 128)
            y = [(slot_obs[8 * i : 8 * i + 8, cols], slot_obs[32 + 8 * i : 40 + 8 * i, cols]) for i in range(4)]
            h = []
            for i in range(4):
                acc = None
                for k in range(4):
                    wr, wi = w[i, k]
                    acc = add_products(acc, (wr[j : j + 1], wi[j : j + 1]), y[k])
                h.append(acc)
            estimates.append(h)
            out = []
            for i in range(4):
                out.append(h[i][0] * h[i][0] + h[i][1] * h[i][1] + err[i, i][0][j : j + 1])
            for i, k in PAIRS:
                out.append(h[i][0] * h[k][0] + h[i][1] * h[k][1] + err[i, k][0][j : j + 1])
                out.append(h[i][1] * h[k][0] - h[i][0] * h[k][1] + err[i, k][1][j : j + 1])
            outers.append(jnp.concatenate(out, 0))
    summed = dot_split(jnp.concatenate(outers, 1), pick, 3, True)
    own_f = lax.broadcasted_iota(jnp.int32, (8, 128), 1) // 16 == lax.broadcasted_iota(jnp.int32, (8, 128), 0)
    comps = [
        jnp.sum(jnp.where(own_f, summed[8 * x : 8 * x + 8], 0.0), 0, keepdims=True) for x in range(16)
    ]
    weight = hermitian_inverse(from_parts([c + 1.0 if x < 4 else c for x, c in enumerate(comps)]))

    masked = jnp.concatenate([jnp.where(own_f, c, 0.0) for c in parts_of(weight)], 0)
    slot_weight = dot_split(masked, pick, 3)
    for g in range(groups):
        cols = slice(128 * g, 128 * g + 128)
        h = estimates[g]
        gs = from_parts([slot_weight[8 * x : 8 * x + 8, cols] for x in range(16)])
        for i in range(4):
            gs[i, i] = (gs[i, i][0], None)
        power = None
        for i in range(4):
            acc = None
            for k in range(4):
                acc = add_products(acc, get(gs, i, k), h[k])
            out_w[g, 8 * i : 8 * i + 8] = acc[0]
            out_w[g, 32 + 8 * i : 40 + 8 * i] = acc[1]
            term = h[i][0] * acc[0] + h[i][1] * acc[1]
            power = term if power is None else power + term
        out_w[g, 64:72] = power
        out_w[g, 72:80] = jnp.broadcast_to(places[:, cols], (8, 128))

        @pl.when(z != g)
        def _():
            w_copy(g, z).start()

    sign = jnp.where(lax.broadcasted_iota(jnp.int32, (8, 128), 1) < 64, 1.0, -1.0)

    def widen(slot, source):
        for s in range(16):
            tile = source(s)
            wide_data[slot, 2 * s] = tile
            wide_data[slot, 2 * s + 1] = pltpu.roll(tile, 64, 1) * sign

    sums = [None] * 8
    power = None
    row16 = lax.broadcasted_iota(jnp.int32, (16, 128), 0).astype(F32)
    in_w[z] = out_w[z]
    for k in range(rows):
        p = z if k == 0 else lax.rem(z + rows - k, rows)
        if k == 0:
            widen(0, lambda s: data[s])
        else:
            data_copy(p, p).wait_recv()
            widen(k, lambda s: data_in[p, s])
            w_copy(p, p).wait_recv()
        vector = in_w[p]
        part = vector[64:72]
        power = part if power is None else power + part
        mask = row16 == vector[72:73]
        heads = vector[0:64].astype(BF16).astype(F32)
        tails = vector[0:64] - heads
        for f in range(8):
            right = jnp.concatenate(
                [
                    jnp.where(mask, x[8 * i + f : 8 * i + f + 1], 0.0)
                    for x in (heads, tails)
                    for i in range(8)
                ],
                0,
            ).astype(BF16)
            hi, lo = split(wide_data[k, :, f, :], 2)
            left = jnp.concatenate(
                [jnp.concatenate([hi, hi], 1), jnp.concatenate([lo, jnp.zeros_like(lo)], 1)], 0
            )
            both = dot(left, right)
            both = both[0:32] + both[32:64]
            sums[f] = both if k == 0 else sums[f] + both
    for half in range(2):
        tile = jnp.concatenate(sums[4 * half : 4 * half + 4], 0).T.reshape(4, 4, 8, 128)
        for j in range(4):
            back[:, 2 * j + half] = tile[j]
    shifted = [power] + [pltpu.roll(power, 128 - 32 * j, 1) for j in range(1, 4)]
    shifted.append(jnp.zeros((96, 128), F32))
    back[:, 8] = jnp.concatenate(shifted, 0).T[0:32].reshape(4, 8, 128)

    for k in range(1, 4):
        back_copy(lax.rem(q + k, 4), q).start()
    home[q] = back[q]
    for k in range(1, 4):
        p = lax.rem(q + 4 - k, 4)
        back_copy(p, p).wait_recv()

    total = (home[0] + home[1]) + (home[2] + home[3])
    for j in range(4):
        for f in range(8):
            tile = total[2 * j + f // 4]
            sym_ref[8 * j : 8 * j + 8, f, :] = tile[:, 32 * (f % 4) : 32 * (f % 4) + 32]
    gains = jnp.concatenate([total[8], jnp.zeros((120, 128), F32)], 0).T
    gain_ref[...] = jnp.concatenate([gains[8 * j : 8 * j + 8, 0:8] for j in range(4)], 1)

    @pl.loop(1, n)
    def _(k):
        p = lax.rem(me + k, n)
        slot_copy(p, p).wait_send()

    @pl.loop(1, rows)
    def _(k):
        p = lax.rem(z + k, rows)
        data_copy(p, p).wait_send()
        w_copy(p, p).wait_send()

    for k in range(1, 4):
        p = lax.rem(q + k, 4)
        back_copy(p, p).wait_send()


def body(n, covariances, clusters, cluster_valid, pilots, received_pilot, received_data):
    vmem = pl.BlockSpec(memory_space=pltpu.VMEM)
    rows = n // 4
    symbols, gain = pl.pallas_call(
        functools.partial(kernel, n),
        out_shape=(
            pltpu.VMEM((32, 8, 32), F32),
            pltpu.VMEM((8, 32), F32),
        ),
        in_specs=[pl.BlockSpec(memory_space=pltpu.HBM)] * 6,
        out_specs=(vmem, vmem),
        scratch_shapes=[
            pltpu.VMEM((32, 512), F32),
            pltpu.VMEM((16, 32), jnp.int32),
            pltpu.VMEM((16, 32), jnp.int32),
            pltpu.VMEM((1, 32), jnp.int32),
            pltpu.VMEM((16, 8, 128), F32),
            pltpu.VMEM((16, 8, 128), F32),
            pltpu.VMEM((n, 8, 128), F32),
            pltpu.VMEM((n, 8, 128), F32),
            pltpu.VMEM((n // 16, 4, 32, 128), F32),
            pltpu.VMEM((4, 16, 128), F32),
            pltpu.VMEM((8, 8, 256), F32),
            pltpu.VMEM((16, 8, 128), F32),
            pltpu.VMEM((rows, 16, 8, 128), F32),
            pltpu.VMEM((rows, 32, 8, 128), F32),
            pltpu.VMEM((rows, 80, 128), F32),
            pltpu.VMEM((rows, 80, 128), F32),
            pltpu.VMEM((4, 9, 8, 128), F32),
            pltpu.VMEM((4, 9, 8, 128), F32),
            pltpu.SemaphoreType.DMA((6,)),
            pltpu.SemaphoreType.DMA((n,)),
            pltpu.SemaphoreType.DMA((n,)),
            pltpu.SemaphoreType.DMA((rows,)),
            pltpu.SemaphoreType.DMA((rows,)),
            pltpu.SemaphoreType.DMA((rows,)),
            pltpu.SemaphoreType.DMA((rows,)),
            pltpu.SemaphoreType.DMA((4,)),
            pltpu.SemaphoreType.DMA((4,)),
        ],
        compiler_params=pltpu.CompilerParams(
            collective_id=0, has_side_effects=True, vmem_limit_bytes=65000 * 1024
        ),
    )(covariances, clusters.T, cluster_valid.T, pilots.reshape(1, -1), received_pilot, received_data)
    return symbols, gain.T


def solution(mesh):
    placed = (
        P("ap", None),
        P("ap", None),
        P("ap", None),
        P("ap"),
        P("ap", "sc", None),
        P("ap", "sc", None),
    )
    return jax.shard_map(
        functools.partial(body, mesh.shape["ap"]),
        mesh=mesh,
        in_specs=placed,
        out_specs=(P("ap", "sc", None), P("ap", "sc")),
        check_vma=False,
    )
```

profile of v0, /device:TPU:0, one launch (start us, length us, event | category | flops | bytes accessed | tf_op | source)
XLA Modules:
  0.0 25.6 jit_solution(12660704612999020283)
XLA Ops:
  0.6 23.7 %shard_map.77 = (f32[32,8,32]{2,1,0:T(8,128)S(1)}, f32[8,32]{1,0:T(8,128)S(1)}) custom-call(f32[32,512]{1,0:T(8,128)} %cov_hbm.1, s32[16,32]{1,0:T(8,128)} %bitcast.5, s32[16,32]{1,0:T(8,128)} %bitcast.6, s32[1,32]{1,0:T(1,128)} %bitcast.7, f32[16,8,128]{2,1,0:T(8,128)} %rp_hbm.1, f32[16,8,128]{2,1,0:T(8,128)} %rd_hbm.1), custom_call_target="tpu_custom_call" | custom-call | tf_op jit(solution)/shard_map/pallas_call | solution.py:435
  24.3 0.7 %copy.10 = f32[32,8,32]{2,1,0:T(8,128)} copy(f32[32,8,32]{2,1,0:T(8,128)S(1)} %get-tuple-element.6) | data formatting | bytes 65536
  25.0 0.6 %copy.11 = f32[32,8]{0,1:T(8,128)} copy(f32[32,8]{0,1:T(8,128)S(1)} %bitcast.4) | data formatting | bytes 2048
where the time goes:
time: 25.8 us; the launch traced here: 25.6 us
  Pallas kernels  23.7 us (92%)
  local copies, waits for them, and re-layouts  1.25 us (5%)
  between operations  0.64 us (2%)
    pallas_call x1, Pallas kernels, body(): pl.pallas_call(functools.partial(kernel, n), out_shape=(pltpu.VMEM((32, 8...  23.7 us
    unnamed x2, local copies, waits for them, and re-layouts  1.25 us

commit v1 on v0

--- a/solution.py
+++ b/solution.py
@@ -12,6 +12,10 @@
 MESH = pl.DeviceIdType.MESH
 PAIRS = [(0, 1), (0, 2), (0, 3), (1, 2), (1, 3), (2, 3)]
 ENTRIES = [(i, i) for i in range(4)] + PAIRS
+DIAGONAL = [8, 11, 9, 12]
+REAL = dict(zip(PAIRS, [0, 1, 2, 3, 4, 10]))
+IMAG = dict(zip(PAIRS, [16, 17, 18, 19, 20, 26]))
+CODE = 24
 
 
 def split(x, parts):
@@ -138,11 +142,11 @@
 
 
 def kernel(
-    n, cov_hbm, cl_hbm, valid_hbm, pilot_hbm, rp_hbm, rd_hbm, sym_ref, gain_ref,
+    n, cov_hbm, cl_hbm, valid_hbm, pilot_hbm, rp_hbm, rd_hbm, home,
     cov_ref, cl_ref, valid_ref, pilot_ref, rp_ref, rd_ref,
-    send, recv, trans, pinv, obs, data, data_in, wide_data, out_w, in_w, back, home,
+    send, recv, trans, pinv, obs, data, data_in, ones, gathered, held, out_p, in_p, out_w, in_w, back,
     load_sem, send_sem, recv_sem, data_send_sem, data_recv_sem,
-    w_send_sem, w_recv_sem, back_send_sem, back_recv_sem,
+    p_send_sem, p_recv_sem, w_send_sem, w_recv_sem, back_send_sem, back_recv_sem,
 ):
     me = lax.axis_index("ap")
     core = lax.axis_index("sc")
@@ -165,35 +169,42 @@
     def _(d):
         pl.semaphore_signal(barrier, inc=1, device_id=(lax.rem(me + d, n), core), device_id_type=MESH)
 
-    lane = lax.broadcasted_iota(jnp.int32, (32, 1024), 1)
-    spread = (lane // 32 == lax.broadcasted_iota(jnp.int32, (32, 1024), 0)).astype(F32).astype(BF16)
-    lane32 = lax.broadcasted_iota(jnp.int32, (32, 512), 1)
-    quarter = lax.broadcasted_iota(jnp.int32, (8, 128), 1) // 32
+    trans[...] = jnp.zeros_like(trans)
+    ones[...] = jnp.zeros_like(ones)
     for load in loads[:4]:
         load.wait()
-    cl = cl_ref[...]
+    wide = lambda x: jnp.concatenate([x] * 4, 1)
+    cl = wide(cl_ref[...])
     code = jnp.where(
-        valid_ref[...] > 0, (pilot_ref[...] * 16 + (cl & 15)).astype(F32) + 1.0, 0.0
+        wide(valid_ref[...]) > 0, (wide(pilot_ref[...]) * 16 + (cl & 15)).astype(F32) + 1.0, 0.0
     )
-    small = jnp.concatenate([(cl >> 4).astype(F32), code], 0).T
-    wide = dot(small.astype(BF16), spread)
-    owner_w, code_w = wide[:, :512], wide[:, 512:]
-    payload = jnp.where((lane32 & 31) == 16, code_w, cov_ref[...])
-    for t in range(n):
-        m = jnp.where(owner_w == float(t), payload, 0.0)
-        s = m[:, 0:128] + m[:, 128:256] + (m[:, 256:384] + m[:, 384:512])
-        s = s + pltpu.roll(s, 64, 1)
-        s = s + pltpu.roll(s, 32, 1)
-        packed = s[0:8]
-        for j in range(1, 4):
-            packed = jnp.where(quarter == j, s[8 * j : 8 * j + 8], packed)
-        send[t] = packed
+    owner = (cl >> 4) - lax.broadcasted_iota(jnp.int32, (16, 128), 1) // 32
+    slots = []
+    for a in range(4):
+        part = cov_ref[:, 128 * a : 128 * a + 128]
+        turned = jnp.concatenate([part] * 4, 0).T
+        slots += [turned[32 * j : 32 * j + 32] for j in range(4)]
+    row8 = lax.broadcasted_iota(jnp.int32, (8, 128), 0)
+    for t in range(n // 4):
+        tiles = [jnp.zeros((8, 128), F32)] * 4
+        mark = jnp.zeros((8, 128), F32)
+        for c in range(16):
+            mine = jnp.broadcast_to(owner[c : c + 1], (8, 128)) == 4 * t
+            tiles = [jnp.where(mine, slots[c][8 * v : 8 * v + 8], tiles[v]) for v in range(4)]
+            mark = jnp.where(mine, jnp.broadcast_to(code[c : c + 1], (8, 128)), mark)
+        first = jnp.broadcast_to(tiles[0][0:1], (8, 128))
+        second = jnp.broadcast_to(tiles[0][5:6], (8, 128))
+        tiles[1] = jnp.where(row8 == 1, first, jnp.where(row8 == 6, second, tiles[1]))
+        tiles[3] = jnp.where(row8 == 1, mark, tiles[3])
+        tiles = [jnp.where(row8 < 3, pltpu.roll(x, 7, 0), pltpu.roll(x, 5, 0)) for x in tiles]
+        for j, tile in enumerate(lane_groups(tiles)):
+            send[4 * t + j] = tile
 
     pl.semaphore_wait(barrier, n - 1)
 
     def slot_copy(p, slot):
         return pltpu.make_async_remote_copy(
-            src_ref=send.at[p], dst_ref=recv.at[slot],
+            src_ref=send.at[p, 0:5], dst_ref=recv.at[slot, 0:5],
             send_sem=send_sem.at[p], recv_sem=recv_sem.at[slot],
             device_id=(p, core), device_id_type=MESH,
         )
@@ -202,6 +213,13 @@
         return pltpu.make_async_remote_copy(
             src_ref=data, dst_ref=data_in.at[slot],
             send_sem=data_send_sem.at[p], recv_sem=data_recv_sem.at[slot],
+            device_id=(q * rows + p, core), device_id_type=MESH,
+        )
+
+    def p_copy(p, slot):
+        return pltpu.make_async_remote_copy(
+            src_ref=out_p.at[p], dst_ref=in_p.at[slot],
+            send_sem=p_send_sem.at[p], recv_sem=p_recv_sem.at[slot],
             device_id=(q * rows + p, core), device_id_type=MESH,
         )
 
@@ -252,11 +270,12 @@
     row32 = lax.broadcasted_iota(jnp.int32, (32, 128), 0)
     codes, matrices = [], []
     for e in range(sets):
-        block = jnp.concatenate([recv[h * rows + 4 * e + l] for l in range(4) for h in range(4)], 0).T
-        for j, tile in enumerate(lane_groups([block[32 * j : 32 * j + 32] for j in range(4)])):
-            trans[e, j] = tile
-            codes.append(tile[16:17])
-            matrices.append(jnp.where(row32 == 16, 0.0, tile))
+        for j in range(4):
+            tiles = lane_groups([recv[h * rows + 4 * e + j] for h in range(4)])
+            for v, tile in enumerate(tiles):
+                trans[e, j, 8 * v : 8 * v + 5] = tile[0:5]
+            codes.append(tiles[3][0:1])
+            matrices.append(jnp.where(row32 == CODE, 0.0, trans[e, j]))
     codes = jnp.concatenate(codes, 1) - 1.0
     matrices = jnp.concatenate(matrices, 1)
     width = 128 * groups
@@ -265,11 +284,16 @@
     places = jnp.where(codes >= 0.0, codes - 16.0 * jnp.floor(codes * 0.0625), -1.0)
     ap_rows = (lax.broadcasted_iota(jnp.int32, (128, width), 0) & 15).astype(F32)
     pick = jnp.where(ap_rows == places, 1.0, 0.0).astype(BF16)
+    for g in range(groups):
+        out_p[g] = jnp.broadcast_to(places[:, 128 * g : 128 * g + 128], (8, 128))
+
+        @pl.when(z != g)
+        def _():
+            p_copy(g, z).start()
 
     psi = dot_split(matrices, choose, 3, True)
-    at = lambda x, i, j: (x[4 * i + j : 4 * i + j + 1], x[16 + 4 * i + j : 17 + 4 * i + j])
-    hermitian = {(i, i): (at(psi, i, i)[0] + 1.0, None) for i in range(4)}
-    hermitian.update({p: at(psi, *p) for p in PAIRS})
+    hermitian = {(i, i): (psi[r : r + 1] + 1.0, None) for i, r in enumerate(DIAGONAL)}
+    hermitian.update({p: (psi[REAL[p] : REAL[p] + 1], psi[IMAG[p] : IMAG[p] + 1]) for p in PAIRS})
     inverse = jnp.concatenate(parts_of(hermitian_inverse(hermitian)), 0)
     slot_inverse = dot_split(inverse, choose, 3)
     slot_obs = dot(observed, choose)
@@ -281,9 +305,9 @@
             g = 4 * e + j
             pinv[j] = slot_inverse[:, 128 * g : 128 * g + 128]
         pi = from_parts([pinv[:, x, :] for x in range(16)])
-        r = {(i, i): (trans[e, :, 5 * i, :], None) for i in range(4)}
-        for i, k in PAIRS:
-            r[i, k] = (trans[e, :, 4 * i + k, :], trans[e, :, 16 + 4 * i + k, :])
+        r = {(i, i): (trans[e, :, DIAGONAL[i], :], None) for i in range(4)}
+        for p in PAIRS:
+            r[p] = (trans[e, :, REAL[p], :], trans[e, :, IMAG[p], :])
         w = {}
         for i in range(4):
             for k in range(4):
@@ -342,61 +366,63 @@
             term = h[i][0] * acc[0] + h[i][1] * acc[1]
             power = term if power is None else power + term
         out_w[g, 64:72] = power
-        out_w[g, 72:80] = jnp.broadcast_to(places[:, cols], (8, 128))
 
         @pl.when(z != g)
         def _():
             w_copy(g, z).start()
 
-    sign = jnp.where(lax.broadcasted_iota(jnp.int32, (8, 128), 1) < 64, 1.0, -1.0)
-
-    def widen(slot, source):
-        for s in range(16):
-            tile = source(s)
-            wide_data[slot, 2 * s] = tile
-            wide_data[slot, 2 * s + 1] = pltpu.roll(tile, 64, 1) * sign
-
-    sums = [None] * 8
-    power = None
     row16 = lax.broadcasted_iota(jnp.int32, (16, 128), 0).astype(F32)
+    in_p[z] = out_p[z]
     in_w[z] = out_w[z]
     for k in range(rows):
-        p = z if k == 0 else lax.rem(z + rows - k, rows)
-        if k == 0:
-            widen(0, lambda s: data[s])
-        else:
+        p = z ^ k
+        if k > 0:
             data_copy(p, p).wait_recv()
-            widen(k, lambda s: data_in[p, s])
+            p_copy(p, p).wait_recv()
+        place = in_p[p]
+        hot = jnp.where(row16 == jnp.concatenate([place, place], 0), 1.0, 0.0).astype(BF16)
+        for i in range(8):
+            for half in range(2):
+                at = 128 * half + 16 * i
+                ones[k % 2, at : at + 16, 128 * i : 128 * i + 128] = hot
+        source = (data[...] if k == 0 else data_in[p]).reshape(128, 128)
+        left = jnp.concatenate(split(source, 2), 1)
+        for i in range(4):
+            cols = slice(256 * i, 256 * i + 256)
+            wide_out = dot(left, ones[k % 2, :, cols])
+            gathered[k, 2 * i] = wide_out[:, :128].reshape(16, 8, 128)
+            gathered[k, 2 * i + 1] = wide_out[:, 128:].reshape(16, 8, 128)
+
+    sums = [None] * 32
+    power = None
+    for k in range(rows):
+        p = z ^ k
+        if k > 0:
             w_copy(p, p).wait_recv()
-        vector = in_w[p]
-        part = vector[64:72]
+        u = [in_w[p, 8 * i : 8 * i + 8] for i in range(8)]
+        part = in_w[p, 64:72]
         power = part if power is None else power + part
-        mask = row16 == vector[72:73]
-        heads = vector[0:64].astype(BF16).astype(F32)
-        tails = vector[0:64] - heads
-        for f in range(8):
-            right = jnp.concatenate(
-                [
-                    jnp.where(mask, x[8 * i + f : 8 * i + f + 1], 0.0)
-                    for x in (heads, tails)
-                    for i in range(8)
-                ],
-                0,
-            ).astype(BF16)
-            hi, lo = split(wide_data[k, :, f, :], 2)
-            left = jnp.concatenate(
-                [jnp.concatenate([hi, hi], 1), jnp.concatenate([lo, jnp.zeros_like(lo)], 1)], 0
-            )
-            both = dot(left, right)
-            both = both[0:32] + both[32:64]
-            sums[f] = both if k == 0 else sums[f] + both
+        for s in range(16):
+            d = [gathered[k, i, s] for i in range(8)]
+            re = im = None
+            for i in range(4):
+                x = u[i] * d[i] + u[i + 4] * d[i + 4]
+                y = u[i] * d[i + 4] - u[i + 4] * d[i]
+                re = x if re is None else re + x
+                im = y if im is None else im + y
+            sums[2 * s] = re if k == 0 else sums[2 * s] + re
+            sums[2 * s + 1] = im if k == 0 else sums[2 * s + 1] + im
+    for s in range(32):
+        held[s] = sums[s]
     for half in range(2):
-        tile = jnp.concatenate(sums[4 * half : 4 * half + 4], 0).T.reshape(4, 4, 8, 128)
+        tile = jnp.concatenate([held[:, 4 * half + f, :] for f in range(4)], 0).T.reshape(4, 4, 8, 128)
         for j in range(4):
-            back[:, 2 * j + half] = tile[j]
-    shifted = [power] + [pltpu.roll(power, 128 - 32 * j, 1) for j in range(1, 4)]
-    shifted.append(jnp.zeros((96, 128), F32))
-    back[:, 8] = jnp.concatenate(shifted, 0).T[0:32].reshape(4, 8, 128)
+            back[:, 2 * j + half] = tile[:, j]
+    turned = jnp.concatenate([power, jnp.zeros((120, 128), F32)], 0).T.reshape(4, 4, 8, 128)
+    gains = turned[:, 0].reshape(32, 128)
+    for j in range(1, 4):
+        gains = gains + pltpu.roll(turned[:, j].reshape(32, 128), 8 * j, 1)
+    back[:, 8] = gains.reshape(4, 8, 128)
 
     for k in range(1, 4):
         back_copy(lax.rem(q + k, 4), q).start()
@@ -405,6 +431,24 @@
         p = lax.rem(q + 4 - k, 4)
         back_copy(p, p).wait_recv()
 
+    @pl.loop(1, n)
+    def _(k):
+        p = lax.rem(me + k, n)
+        slot_copy(p, p).wait_send()
+
+    @pl.loop(1, rows)
+    def _(k):
+        p = lax.rem(z + k, rows)
+        data_copy(p, p).wait_send()
+        p_copy(p, p).wait_send()
+        w_copy(p, p).wait_send()
+
+    for k in range(1, 4):
+        p = lax.rem(q + k, 4)
+        back_copy(p, p).wait_send()
+
+
+def finish(home, sym_ref, gain_ref):
     total = (home[0] + home[1]) + (home[2] + home[3])
     for j in range(4):
         for f in range(8):
@@ -413,33 +457,15 @@
     gains = jnp.concatenate([total[8], jnp.zeros((120, 128), F32)], 0).T
     gain_ref[...] = jnp.concatenate([gains[8 * j : 8 * j + 8, 0:8] for j in range(4)], 1)
 
-    @pl.loop(1, n)
-    def _(k):
-        p = lax.rem(me + k, n)
-        slot_copy(p, p).wait_send()
-
-    @pl.loop(1, rows)
-    def _(k):
-        p = lax.rem(z + k, rows)
-        data_copy(p, p).wait_send()
-        w_copy(p, p).wait_send()
-
-    for k in range(1, 4):
-        p = lax.rem(q + k, 4)
-        back_copy(p, p).wait_send()
-
 
 def body(n, covariances, clusters, cluster_valid, pilots, received_pilot, received_data):
     vmem = pl.BlockSpec(memory_space=pltpu.VMEM)
     rows = n // 4
-    symbols, gain = pl.pallas_call(
+    home = pl.pallas_call(
         functools.partial(kernel, n),
-        out_shape=(
-            pltpu.VMEM((32, 8, 32), F32),
-            pltpu.VMEM((8, 32), F32),
-        ),
+        out_shape=pltpu.VMEM((4, 9, 8, 128), F32),
         in_specs=[pl.BlockSpec(memory_space=pltpu.HBM)] * 6,
-        out_specs=(vmem, vmem),
+        out_specs=vmem,
         scratch_shapes=[
             pltpu.VMEM((32, 512), F32),
             pltpu.VMEM((16, 32), jnp.int32),
@@ -454,14 +480,19 @@
             pltpu.VMEM((8, 8, 256), F32),
             pltpu.VMEM((16, 8, 128), F32),
             pltpu.VMEM((rows, 16, 8, 128), F32),
-            pltpu.VMEM((rows, 32, 8, 128), F32),
-            pltpu.VMEM((rows, 80, 128), F32),
-            pltpu.VMEM((rows, 80, 128), F32),
-            pltpu.VMEM((4, 9, 8, 128), F32),
+            pltpu.VMEM((2, 256, 1024), BF16),
+            pltpu.VMEM((rows, 8, 16, 8, 128), F32),
+            pltpu.VMEM((32, 8, 128), F32),
+            pltpu.VMEM((rows, 8, 128), F32),
+            pltpu.VMEM((rows, 8, 128), F32),
+            pltpu.VMEM((rows, 72, 128), F32),
+            pltpu.VMEM((rows, 72, 128), F32),
             pltpu.VMEM((4, 9, 8, 128), F32),
             pltpu.SemaphoreType.DMA((6,)),
             pltpu.SemaphoreType.DMA((n,)),
             pltpu.SemaphoreType.DMA((n,)),
+            pltpu.SemaphoreType.DMA((rows,)),
+            pltpu.SemaphoreType.DMA((rows,)),
             pltpu.SemaphoreType.DMA((rows,)),
             pltpu.SemaphoreType.DMA((rows,)),
             pltpu.SemaphoreType.DMA((rows,)),
@@ -473,6 +504,12 @@
             collective_id=0, has_side_effects=True, vmem_limit_bytes=65000 * 1024
         ),
     )(covariances, clusters.T, cluster_valid.T, pilots.reshape(1, -1), received_pilot, received_data)
+    symbols, gain = pl.pallas_call(
+        finish,
+        out_shape=(jax.ShapeDtypeStruct((32, 8, 32), F32), jax.ShapeDtypeStruct((8, 32), F32)),
+        in_specs=[vmem],
+        out_specs=(vmem, vmem),
+    )(pltpu.with_memory_space_constraint(home, pltpu.VMEM))
     return symbols, gain.T
 
 

time: 25.8 us -> 23.3 us (0.903)
  local copies, waits for them, and re-layouts: 1.25 us -> 0 us
  Pallas kernels: 23.7 us -> 22.5 us
    unnamed x2 -> x0, local copies, waits for them, and re-layouts: 1.25 us -> none
    pallas_call x1 -> x2, Pallas kernels: 23.7 us -> 22.5 us  [the longest x1 21.5 us: body(): pl.pallas_call(functools.partial(kernel, n), out_shape=pltpu.VMEM((4, 9,...]
where the time goes in v1:
time: 23.3 us; the launch traced here: 23.1 us
  Pallas kernels  22.5 us (97%)
  between operations  0.64 us (3%)
    pallas_call x1, Pallas kernels, body(): pl.pallas_call(functools.partial(kernel, n), out_shape=pltpu.VMEM((4, 9,...  21.5 us
    pallas_call x1, Pallas kernels, body(): pl.pallas_call(finish, out_shape=(jax.ShapeDtypeStruct((32, 8, 32), F32),...  0.96 us

profile of v1, /device:TPU:0, one launch (start us, length us, event | category | flops | bytes accessed | tf_op | source)
XLA Modules:
  0.0 23.1 jit_solution(9576760781281499370)
XLA Ops:
  0.6 21.5 %shard_map.77.home = f32[4,9,8,128]{3,2,1,0:T(8,128)S(1)} custom-call(f32[32,512]{1,0:T(8,128)} %cov_hbm.1, s32[16,32]{1,0:T(8,128)} %bitcast.4, s32[16,32]{1,0:T(8,128)} %bitcast.5, s32[1,32]{1,0:T(1,128)} %bitcast.6, f32[16,8,128]{2,1,0:T(8,128)} %rp_hbm.1, f32[16,8,128]{2,1,0:T(8,128)} %rd_hbm.1), custom_call_target="tpu_custom_call" | custom-call | tf_op jit(solution)/shard_map/pallas_call | solution.py:464
  22.2 1.0 %shard_map.78 = (f32[32,8,32]{2,1,0:T(8,128)}, f32[8,32]{1,0:T(8,128)}) custom-call(f32[4,9,8,128]{3,2,1,0:T(8,128)S(1)} %shard_map.77.home), custom_call_target="tpu_custom_call" | custom-call | tf_op jit(solution)/shard_map/pallas_call | solution.py:507

commit v2 on v1

--- a/solution.py
+++ b/solution.py
@@ -160,53 +160,46 @@
         (cov_hbm, cov_ref), (rp_hbm, rp_ref), (rd_hbm, rd_ref),
     ]
     loads = [pltpu.make_async_copy(a, b, load_sem.at[i]) for i, (a, b) in enumerate(pairs)]
-    for load in loads:
+    odd = lax.rem(core, 2) == 1
+    pair = core ^ 1
+    barrier = pltpu.get_barrier_semaphore()
+
+    def greet(p, c):
+        pl.semaphore_signal(barrier, inc=1, device_id=(p, c), device_id_type=MESH)
+
+    @pl.when(odd)
+    def _():
+        for load in loads[:4]:
+            load.start()
+
+        @pl.loop(1, n)
+        def _(d):
+            greet(me ^ (n - d), core)
+
+    @pl.when(jnp.logical_not(odd))
+    def _():
+        @pl.loop(0, n)
+        def _(d):
+            greet(me ^ (n - 1 - d), pair)
+
+        @pl.loop(1, rows)
+        def _(d):
+            greet(q * rows + (z ^ d), core)
+
+        for d in range(1, 4):
+            greet((q ^ d) * rows + z, core)
+
+    for load in loads[4:]:
         load.start()
-
-    barrier = pltpu.get_barrier_semaphore()
-
-    @pl.loop(1, n)
-    def _(d):
-        pl.semaphore_signal(barrier, inc=1, device_id=(lax.rem(me + d, n), core), device_id_type=MESH)
 
     trans[...] = jnp.zeros_like(trans)
     ones[...] = jnp.zeros_like(ones)
-    for load in loads[:4]:
-        load.wait()
-    wide = lambda x: jnp.concatenate([x] * 4, 1)
-    cl = wide(cl_ref[...])
-    code = jnp.where(
-        wide(valid_ref[...]) > 0, (wide(pilot_ref[...]) * 16 + (cl & 15)).astype(F32) + 1.0, 0.0
-    )
-    owner = (cl >> 4) - lax.broadcasted_iota(jnp.int32, (16, 128), 1) // 32
-    slots = []
-    for a in range(4):
-        part = cov_ref[:, 128 * a : 128 * a + 128]
-        turned = jnp.concatenate([part] * 4, 0).T
-        slots += [turned[32 * j : 32 * j + 32] for j in range(4)]
-    row8 = lax.broadcasted_iota(jnp.int32, (8, 128), 0)
-    for t in range(n // 4):
-        tiles = [jnp.zeros((8, 128), F32)] * 4
-        mark = jnp.zeros((8, 128), F32)
-        for c in range(16):
-            mine = jnp.broadcast_to(owner[c : c + 1], (8, 128)) == 4 * t
-            tiles = [jnp.where(mine, slots[c][8 * v : 8 * v + 8], tiles[v]) for v in range(4)]
-            mark = jnp.where(mine, jnp.broadcast_to(code[c : c + 1], (8, 128)), mark)
-        first = jnp.broadcast_to(tiles[0][0:1], (8, 128))
-        second = jnp.broadcast_to(tiles[0][5:6], (8, 128))
-        tiles[1] = jnp.where(row8 == 1, first, jnp.where(row8 == 6, second, tiles[1]))
-        tiles[3] = jnp.where(row8 == 1, mark, tiles[3])
-        tiles = [jnp.where(row8 < 3, pltpu.roll(x, 7, 0), pltpu.roll(x, 5, 0)) for x in tiles]
-        for j, tile in enumerate(lane_groups(tiles)):
-            send[4 * t + j] = tile
-
-    pl.semaphore_wait(barrier, n - 1)
-
-    def slot_copy(p, slot):
+
+    def slot_copy(p, slot, to):
         return pltpu.make_async_remote_copy(
             src_ref=send.at[p, 0:5], dst_ref=recv.at[slot, 0:5],
-            send_sem=send_sem.at[p], recv_sem=recv_sem.at[slot],
-            device_id=(p, core), device_id_type=MESH,
+            send_sem=send_sem.at[lax.rem(to, 2), p], recv_sem=recv_sem.at[slot],
+            device_id=(p, to), device_id_type=MESH,
         )
 
     def data_copy(p, slot):
@@ -237,12 +230,51 @@
             device_id=(p * rows + z, core), device_id_type=MESH,
         )
 
-    @pl.loop(1, n)
-    def _(d):
-        p = lax.rem(me + d, n)
-        slot_copy(p, me).start()
-
-    recv[me] = send[me]
+    @pl.when(odd)
+    def _():
+        for load in loads[:4]:
+            load.wait()
+        wide = lambda x: jnp.concatenate([x] * 4, 1)
+        cl = wide(cl_ref[...])
+        code = jnp.where(
+            wide(valid_ref[...]) > 0, (wide(pilot_ref[...]) * 16 + (cl & 15)).astype(F32) + 1.0, 0.0
+        )
+        owner = (cl >> 4) - lax.broadcasted_iota(jnp.int32, (16, 128), 1) // 32
+        slots = []
+        for a in range(4):
+            part = cov_ref[:, 128 * a : 128 * a + 128]
+            turned = jnp.concatenate([part] * 4, 0).T
+            slots += [turned[32 * j : 32 * j + 32] for j in range(4)]
+        row8 = lax.broadcasted_iota(jnp.int32, (8, 128), 0)
+        for t in range(n // 4):
+            tiles = [jnp.zeros((8, 128), F32)] * 4
+            mark = jnp.zeros((8, 128), F32)
+            for c in range(16):
+                mine = jnp.broadcast_to(owner[c : c + 1], (8, 128)) == 4 * t
+                tiles = [jnp.where(mine, slots[c][8 * v : 8 * v + 8], tiles[v]) for v in range(4)]
+                mark = jnp.where(mine, jnp.broadcast_to(code[c : c + 1], (8, 128)), mark)
+            first = jnp.broadcast_to(tiles[0][0:1], (8, 128))
+            second = jnp.broadcast_to(tiles[0][5:6], (8, 128))
+            tiles[1] = jnp.where(row8 == 1, first, jnp.where(row8 == 6, second, tiles[1]))
+            tiles[3] = jnp.where(row8 == 1, mark, tiles[3])
+            tiles = [jnp.where(row8 < 3, pltpu.roll(x, 7, 0), pltpu.roll(x, 5, 0)) for x in tiles]
+            for j, tile in enumerate(lane_groups(tiles)):
+                send[4 * t + j] = tile
+        pl.semaphore_wait(barrier, 2 * n - 1)
+
+        @pl.loop(0, n)
+        def _(d):
+            slot_copy(me ^ (n - 1 - d), me, pair).start()
+
+        @pl.loop(1, n)
+        def _(d):
+            slot_copy(me ^ (n - d), me, core).start()
+
+        recv[me] = send[me]
+
+    @pl.when(jnp.logical_not(odd))
+    def _():
+        pl.semaphore_wait(barrier, rows + 2)
 
     for load in loads[4:]:
         load.wait()
@@ -264,8 +296,13 @@
 
     @pl.loop(1, n)
     def _(d):
-        p = lax.rem(me + n - d, n)
-        slot_copy(p, p).wait_recv()
+        p = me ^ d
+        slot_copy(p, p, pair).wait_recv()
+
+    @pl.when(jnp.logical_not(odd))
+    def _():
+        slot_copy(me, me, pair).wait_recv()
+
 
     row32 = lax.broadcasted_iota(jnp.int32, (32, 128), 0)
     codes, matrices = [], []
@@ -431,10 +468,15 @@
         p = lax.rem(q + 4 - k, 4)
         back_copy(p, p).wait_recv()
 
-    @pl.loop(1, n)
-    def _(k):
-        p = lax.rem(me + k, n)
-        slot_copy(p, p).wait_send()
+    @pl.when(odd)
+    def _():
+        @pl.loop(1, n)
+        def _(k):
+            p = me ^ k
+            slot_copy(p, p, pair).wait_send()
+            slot_copy(p, p, core).wait_send()
+
+        slot_copy(me, me, pair).wait_send()
 
     @pl.loop(1, rows)
     def _(k):
@@ -489,7 +531,7 @@
             pltpu.VMEM((rows, 72, 128), F32),
             pltpu.VMEM((4, 9, 8, 128), F32),
             pltpu.SemaphoreType.DMA((6,)),
-            pltpu.SemaphoreType.DMA((n,)),
+            pltpu.SemaphoreType.DMA((2, n)),
             pltpu.SemaphoreType.DMA((n,)),
             pltpu.SemaphoreType.DMA((rows,)),
             pltpu.SemaphoreType.DMA((rows,)),

time: 23.3 us -> 22.7 us (0.974)
  Pallas kernels: 22.5 us -> 21.9 us
    pallas_call x1, Pallas kernels: 21.5 us -> 21 us  [body(): pl.pallas_call(functools.partial(kernel, n), out_shape=pltpu.VMEM((4, 9,...]
where the time goes in v2:
time: 22.7 us; the launch traced here: 22.6 us
  Pallas kernels  21.9 us (96%)
  between operations  0.64 us (3%)
    pallas_call x1, Pallas kernels, body(): pl.pallas_call(functools.partial(kernel, n), out_shape=pltpu.VMEM((4, 9,...  21 us
    pallas_call x1, Pallas kernels, body(): pl.pallas_call(finish, out_shape=(jax.ShapeDtypeStruct((32, 8, 32), F32),...  0.96 us

profile of v2, /device:TPU:0, one launch (start us, length us, event | category | flops | bytes accessed | tf_op | source)
XLA Modules:
  0.0 22.6 jit_solution(11033643050175332279)
XLA Ops:
  0.6 21.0 %shard_map.77.home = f32[4,9,8,128]{3,2,1,0:T(8,128)S(1)} custom-call(f32[32,512]{1,0:T(8,128)} %cov_hbm.1, s32[16,32]{1,0:T(8,128)} %bitcast.4, s32[16,32]{1,0:T(8,128)} %bitcast.5, s32[1,32]{1,0:T(1,128)} %bitcast.6, f32[16,8,128]{2,1,0:T(8,128)} %rp_hbm.1, f32[16,8,128]{2,1,0:T(8,128)} %rd_hbm.1), custom_call_target="tpu_custom_call" | custom-call | tf_op jit(solution)/shard_map/pallas_call | solution.py:506
  21.6 1.0 %shard_map.78 = (f32[32,8,32]{2,1,0:T(8,128)}, f32[8,32]{1,0:T(8,128)}) custom-call(f32[4,9,8,128]{3,2,1,0:T(8,128)S(1)} %shard_map.77.home), custom_call_target="tpu_custom_call" | custom-call | tf_op jit(solution)/shard_map/pallas_call | solution.py:549

commit v3 on v2

--- a/solution.py
+++ b/solution.py
@@ -145,8 +145,10 @@
     n, cov_hbm, cl_hbm, valid_hbm, pilot_hbm, rp_hbm, rd_hbm, home,
     cov_ref, cl_ref, valid_ref, pilot_ref, rp_ref, rd_ref,
     send, recv, trans, pinv, obs, data, data_in, ones, gathered, held, out_p, in_p, out_w, in_w, back,
+    root_data, root_held, out_r, root_in,
     load_sem, send_sem, recv_sem, data_send_sem, data_recv_sem,
     p_send_sem, p_recv_sem, w_send_sem, w_recv_sem, back_send_sem, back_recv_sem,
+    root_send_sem, root_data_sem, root_recv_sem,
 ):
     me = lax.axis_index("ap")
     core = lax.axis_index("sc")
@@ -162,6 +164,9 @@
     loads = [pltpu.make_async_copy(a, b, load_sem.at[i]) for i, (a, b) in enumerate(pairs)]
     odd = lax.rem(core, 2) == 1
     pair = core ^ 1
+    even = jnp.logical_not(odd)
+    root = jnp.logical_and(me == 0, even)
+    far = jnp.logical_and(q == 3, even)
     barrier = pltpu.get_barrier_semaphore()
 
     def greet(p, c):
@@ -188,6 +193,15 @@
 
         for d in range(1, 4):
             greet((q ^ d) * rows + z, core)
+
+    @pl.when(root)
+    def _():
+        for load in loads[:2]:
+            load.start()
+
+        @pl.loop(1, rows)
+        def _(c):
+            greet(3 * rows + c, core)
 
     for load in loads[4:]:
         load.start()
@@ -221,6 +235,20 @@
             src_ref=out_w.at[p], dst_ref=in_w.at[slot],
             send_sem=w_send_sem.at[p], recv_sem=w_recv_sem.at[slot],
             device_id=(q * rows + p, core), device_id_type=MESH,
+        )
+
+    def root_data_copy(slot):
+        return pltpu.make_async_remote_copy(
+            src_ref=data, dst_ref=root_data.at[slot],
+            send_sem=root_send_sem.at[0], recv_sem=root_data_sem.at[slot],
+            device_id=(0, core), device_id_type=MESH,
+        )
+
+    def root_copy(slot):
+        return pltpu.make_async_remote_copy(
+            src_ref=out_r, dst_ref=root_in.at[slot],
+            send_sem=root_send_sem.at[1], recv_sem=root_recv_sem.at[slot],
+            device_id=(0, core), device_id_type=MESH,
         )
 
     def back_copy(p, slot):
@@ -272,7 +300,13 @@
 
         recv[me] = send[me]
 
-    @pl.when(jnp.logical_not(odd))
+    extra = jnp.logical_and(far, z > 0)
+
+    @pl.when(jnp.logical_and(even, extra))
+    def _():
+        pl.semaphore_wait(barrier, rows + 3)
+
+    @pl.when(jnp.logical_and(even, jnp.logical_not(extra)))
     def _():
         pl.semaphore_wait(barrier, rows + 2)
 
@@ -285,6 +319,10 @@
     @pl.loop(1, rows)
     def _(d):
         data_copy(lax.rem(z + d, rows), z).start()
+
+    @pl.when(far)
+    def _():
+        root_data_copy(z).start()
 
     turned = jnp.concatenate([rp_ref[:, f, :] for f in range(8)], 0).T
     for half in range(2):
@@ -404,6 +442,19 @@
             power = term if power is None else power + term
         out_w[g, 64:72] = power
 
+        if g == 0:
+            @pl.when(far)
+            def _():
+                quarter = lax.broadcasted_iota(jnp.int32, (8, 128), 1) // 32
+                for m in range(2):
+                    packed = out_w[0, 32 * m : 32 * m + 8]
+                    for j in range(1, 4):
+                        at = 32 * m + 8 * j
+                        packed = jnp.where(quarter == j, pltpu.roll(out_w[0, at : at + 8], 32 * j, 1), packed)
+                    out_r[8 * m : 8 * m + 8] = packed
+                out_r[16:24] = out_w[0, 64:72]
+                root_copy(z).start()
+
         @pl.when(z != g)
         def _():
             w_copy(g, z).start()
@@ -461,12 +512,67 @@
         gains = gains + pltpu.roll(turned[:, j].reshape(32, 128), 8 * j, 1)
     back[:, 8] = gains.reshape(4, 8, 128)
 
+    to_root = lambda p: jnp.logical_and(p == 0, jnp.logical_and(z == 0, far))
     for k in range(1, 4):
-        back_copy(lax.rem(q + k, 4), q).start()
+        p = lax.rem(q + k, 4)
+
+        @pl.when(jnp.logical_not(to_root(p)))
+        def _():
+            back_copy(p, q).start()
+
+    @pl.when(root)
+    def _():
+        for load in loads[:2]:
+            load.wait()
+        cl = jnp.concatenate([cl_ref[...]] * 4, 1)
+        valid = jnp.concatenate([valid_ref[...]] * 4, 1)
+        mark = jnp.where(valid > 0, (cl & 15).astype(F32) + 1.0, 0.0)
+        owner = cl >> 4
+        row = lax.broadcasted_iota(jnp.int32, (128, 128), 0)
+        quarter = lax.broadcasted_iota(jnp.int32, (128, 128), 1) // 32
+        base = jnp.where(((row >> 4) & 3) == quarter, ((row & 15) + 1).astype(F32), -1.0)
+        for p in range(rows):
+            place = jnp.sum(jnp.where(owner == 3 * rows + p, mark, 0.0), 0, keepdims=True)
+            hot = jnp.where(base == place, 1.0, 0.0)
+            hot = jnp.concatenate(
+                [jnp.where(row < 64, hot, 0.0), jnp.where(row < 64, 0.0, hot)], 1
+            ).astype(BF16)
+            root_data_copy(p).wait_recv()
+            left = jnp.concatenate(split(root_data[p].reshape(128, 128), 2), 1)
+            both = dot(left, jnp.concatenate([hot, hot], 0))
+            for m in range(2):
+                root_held[p, m] = both[:, 128 * m : 128 * m + 128].reshape(16, 8, 128)
+        sums = [None] * 32
+        power = None
+        for p in range(rows):
+            root_copy(p).wait_recv()
+            u, v, part = (root_in[p, 8 * m : 8 * m + 8] for m in range(3))
+            power = part if p == 0 else power + part
+            for s in range(16):
+                x, y = root_held[p, 0, s], root_held[p, 1, s]
+                re, im = u * x + v * y, u * y - v * x
+                sums[2 * s] = re if p == 0 else sums[2 * s] + re
+                sums[2 * s + 1] = im if p == 0 else sums[2 * s + 1] + im
+        for s in range(32):
+            x = sums[s] + pltpu.roll(sums[s], 64, 1)
+            held[s] = x + pltpu.roll(x, 32, 1)
+        for half in range(2):
+            tile = jnp.concatenate([held[:, 4 * half + f, :] for f in range(4)], 0).T
+            for j in range(4):
+                home[3, 2 * j + half] = tile[8 * j : 8 * j + 8]
+        turned = jnp.concatenate([power, jnp.zeros((120, 128), F32)], 0).T
+        gains = turned[0:8]
+        for j in range(1, 4):
+            gains = gains + pltpu.roll(turned[8 * j : 8 * j + 8], 8 * j, 1)
+        home[3, 8] = gains
+
     home[q] = back[q]
     for k in range(1, 4):
-        p = lax.rem(q + 4 - k, 4)
-        back_copy(p, p).wait_recv()
+        p = lax.rem(q + k, 4)
+
+        @pl.when(jnp.logical_not(jnp.logical_and(root, p == 3)))
+        def _():
+            back_copy(p, p).wait_recv()
 
     @pl.when(odd)
     def _():
@@ -487,7 +593,15 @@
 
     for k in range(1, 4):
         p = lax.rem(q + k, 4)
-        back_copy(p, p).wait_send()
+
+        @pl.when(jnp.logical_not(to_root(p)))
+        def _():
+            back_copy(p, p).wait_send()
+
+    @pl.when(far)
+    def _():
+        root_data_copy(z).wait_send()
+        root_copy(z).wait_send()
 
 
 def finish(home, sym_ref, gain_ref):
@@ -530,6 +644,10 @@
             pltpu.VMEM((rows, 72, 128), F32),
             pltpu.VMEM((rows, 72, 128), F32),
             pltpu.VMEM((4, 9, 8, 128), F32),
+            pltpu.VMEM((rows, 16, 8, 128), F32),
+            pltpu.VMEM((rows, 2, 16, 8, 128), F32),
+            pltpu.VMEM((24, 128), F32),
+            pltpu.VMEM((rows, 24, 128), F32),
             pltpu.SemaphoreType.DMA((6,)),
             pltpu.SemaphoreType.DMA((2, n)),
             pltpu.SemaphoreType.DMA((n,)),
@@ -541,6 +659,9 @@
             pltpu.SemaphoreType.DMA((rows,)),
             pltpu.SemaphoreType.DMA((4,)),
             pltpu.SemaphoreType.DMA((4,)),
+            pltpu.SemaphoreType.DMA((2,)),
+            pltpu.SemaphoreType.DMA((rows,)),
+            pltpu.SemaphoreType.DMA((rows,)),
         ],
         compiler_params=pltpu.CompilerParams(
             collective_id=0, has_side_effects=True, vmem_limit_bytes=65000 * 1024

time: 22.7 us -> 22.1 us (0.974)
  Pallas kernels: 21.9 us -> 21.3 us
    pallas_call x1, Pallas kernels: 21 us -> 20.4 us  [body(): pl.pallas_call(functools.partial(kernel, n), out_shape=pltpu.VMEM((4, 9,...]
where the time goes in v3:
time: 22.1 us; the launch traced here: 22 us
  Pallas kernels  21.3 us (96%)
  between operations  0.64 us (3%)
    pallas_call x1, Pallas kernels, body(): pl.pallas_call(functools.partial(kernel, n), out_shape=pltpu.VMEM((4, 9,...  20.4 us
    pallas_call x1, Pallas kernels, body(): pl.pallas_call(finish, out_shape=(jax.ShapeDtypeStruct((32, 8, 32), F32),...  0.96 us

profile of v3, /device:TPU:0, one launch (start us, length us, event | category | flops | bytes accessed | tf_op | source)
XLA Modules:
  0.0 22.0 jit_solution(18172443308184658607)
XLA Ops:
  0.6 20.4 %shard_map.77.home = f32[4,9,8,128]{3,2,1,0:T(8,128)S(1)} custom-call(f32[32,512]{1,0:T(8,128)} %cov_hbm.1, s32[16,32]{1,0:T(8,128)} %bitcast.4, s32[16,32]{1,0:T(8,128)} %bitcast.5, s32[1,32]{1,0:T(1,128)} %bitcast.6, f32[16,8,128]{2,1,0:T(8,128)} %rp_hbm.1, f32[16,8,128]{2,1,0:T(8,128)} %rd_hbm.1), custom_call_target="tpu_custom_call" | custom-call | tf_op jit(solution)/shard_map/pallas_call | solution.py:620
  21.0 1.0 %shard_map.78 = (f32[32,8,32]{2,1,0:T(8,128)}, f32[8,32]{1,0:T(8,128)}) custom-call(f32[4,9,8,128]{3,2,1,0:T(8,128)S(1)} %shard_map.77.home), custom_call_target="tpu_custom_call" | custom-call | tf_op jit(solution)/shard_map/pallas_call | solution.py:670

commit v4 on v3

--- a/solution.py
+++ b/solution.py
@@ -78,13 +78,6 @@
     return {k: (-v[0], None if v[1] is None else -v[1]) for k, v in h.items()}
 
 
-def parts_of(h):
-    out = [h[i, i][0] for i in range(4)]
-    for p in PAIRS:
-        out += list(h[p])
-    return out
-
-
 def from_parts(x):
     h = {(i, i): (x[i], None) for i in range(4)}
     for q, p in enumerate(PAIRS):
@@ -366,11 +359,18 @@
         def _():
             p_copy(g, z).start()
 
-    psi = dot_split(matrices, choose, 3, True)
-    hermitian = {(i, i): (psi[r : r + 1] + 1.0, None) for i, r in enumerate(DIAGONAL)}
-    hermitian.update({p: (psi[REAL[p] : REAL[p] + 1], psi[IMAG[p] : IMAG[p] + 1]) for p in PAIRS})
-    inverse = jnp.concatenate(parts_of(hermitian_inverse(hermitian)), 0)
-    slot_inverse = dot_split(inverse, choose, 3)
+    if sets == 1:
+        rest = jnp.zeros((124, 128), F32)
+        column = jnp.concatenate([codes[:, 128 * j : 128 * j + 128] for j in range(4)] + [rest], 0).T
+        column_places = jnp.where(column >= 0.0, column - 16.0 * jnp.floor(column * 0.0625), -1.0)
+
+        def alike(x, y):
+            blocks = [jnp.where(x[:, j : j + 1] == y, 1.0, 0.0).astype(BF16) for j in range(4)]
+            return jnp.concatenate(blocks, 0)
+
+        slot_psi = dot_split(matrices, alike(column, codes), 3)
+    else:
+        slot_psi = dot_split(dot_split(matrices, choose, 3, True), choose, 3)
     slot_obs = dot(observed, choose)
     slot_obs = slot_obs[0:64] + slot_obs[64:128] + slot_obs[128:192]
 
@@ -378,8 +378,10 @@
     for e in range(sets):
         for j in range(4):
             g = 4 * e + j
-            pinv[j] = slot_inverse[:, 128 * g : 128 * g + 128]
-        pi = from_parts([pinv[:, x, :] for x in range(16)])
+            pinv[j] = slot_psi[:, 128 * g : 128 * g + 128]
+        psi = {(i, i): (pinv[:, DIAGONAL[i], :] + 1.0, None) for i in range(4)}
+        psi.update({p: (pinv[:, REAL[p], :], pinv[:, IMAG[p], :]) for p in PAIRS})
+        pi = hermitian_inverse(psi)
         r = {(i, i): (trans[e, :, DIAGONAL[i], :], None) for i in range(4)}
         for p in PAIRS:
             r[p] = (trans[e, :, REAL[p], :], trans[e, :, IMAG[p], :])
@@ -416,21 +418,22 @@
                 out.append(h[i][0] * h[k][0] + h[i][1] * h[k][1] + err[i, k][0][j : j + 1])
                 out.append(h[i][1] * h[k][0] - h[i][0] * h[k][1] + err[i, k][1][j : j + 1])
             outers.append(jnp.concatenate(out, 0))
-    summed = dot_split(jnp.concatenate(outers, 1), pick, 3, True)
-    own_f = lax.broadcasted_iota(jnp.int32, (8, 128), 1) // 16 == lax.broadcasted_iota(jnp.int32, (8, 128), 0)
-    comps = [
-        jnp.sum(jnp.where(own_f, summed[8 * x : 8 * x + 8], 0.0), 0, keepdims=True) for x in range(16)
-    ]
-    weight = hermitian_inverse(from_parts([c + 1.0 if x < 4 else c for x, c in enumerate(comps)]))
-
-    masked = jnp.concatenate([jnp.where(own_f, c, 0.0) for c in parts_of(weight)], 0)
-    slot_weight = dot_split(masked, pick, 3)
+    outers = jnp.concatenate(outers, 1)
+    if sets == 1:
+        slot_sum = dot_split(outers, alike(column_places, places), 3)
+    else:
+        summed = dot_split(outers, pick, 3, True)
+        own_f = lax.broadcasted_iota(jnp.int32, (8, 128), 1) // 16 == lax.broadcasted_iota(jnp.int32, (8, 128), 0)
+        comps = [
+            jnp.sum(jnp.where(own_f, summed[8 * x : 8 * x + 8], 0.0), 0, keepdims=True) for x in range(16)
+        ]
+        masked = jnp.concatenate([jnp.where(own_f, c, 0.0) for c in comps], 0)
+        slot_sum = dot_split(masked, pick, 3)
     for g in range(groups):
         cols = slice(128 * g, 128 * g + 128)
         h = estimates[g]
-        gs = from_parts([slot_weight[8 * x : 8 * x + 8, cols] for x in range(16)])
-        for i in range(4):
-            gs[i, i] = (gs[i, i][0], None)
+        parts = [slot_sum[8 * x : 8 * x + 8, cols] for x in range(16)]
+        gs = hermitian_inverse(from_parts([c + 1.0 if x < 4 else c for x, c in enumerate(parts)]))
         power = None
         for i in range(4):
             acc = None
@@ -513,10 +516,10 @@
     back[:, 8] = gains.reshape(4, 8, 128)
 
     to_root = lambda p: jnp.logical_and(p == 0, jnp.logical_and(z == 0, far))
-    for k in range(1, 4):
-        p = lax.rem(q + k, 4)
-
-        @pl.when(jnp.logical_not(to_root(p)))
+    for p in range(4):
+        here = jnp.logical_or(q == p, to_root(p))
+
+        @pl.when(jnp.logical_not(here))
         def _():
             back_copy(p, q).start()
 
@@ -632,7 +635,7 @@
             pltpu.VMEM((n, 8, 128), F32),
             pltpu.VMEM((n, 8, 128), F32),
             pltpu.VMEM((n // 16, 4, 32, 128), F32),
-            pltpu.VMEM((4, 16, 128), F32),
+            pltpu.VMEM((4, 32, 128), F32),
             pltpu.VMEM((8, 8, 256), F32),
             pltpu.VMEM((16, 8, 128), F32),
             pltpu.VMEM((rows, 16, 8, 128), F32),

time: 22.1 us -> 21.9 us (level)
  no operation moved by 1% of the time
where the time goes in v4:
time: 21.9 us; the launch traced here: 21.8 us
  Pallas kernels  21.1 us (96%)
  between operations  0.64 us (3%)
    pallas_call x1, Pallas kernels, body(): pl.pallas_call(functools.partial(kernel, n), out_shape=pltpu.VMEM((4, 9,...  20.2 us
    pallas_call x1, Pallas kernels, body(): pl.pallas_call(finish, out_shape=(jax.ShapeDtypeStruct((32, 8, 32), F32),...  0.96 us

profile of v4, /device:TPU:0, one launch (start us, length us, event | category | flops | bytes accessed | tf_op | source)
XLA Modules:
  0.0 21.8 jit_solution(6240414421138863542)
XLA Ops:
  0.6 20.2 %shard_map.77.home = f32[4,9,8,128]{3,2,1,0:T(8,128)S(1)} custom-call(f32[32,512]{1,0:T(8,128)} %cov_hbm.1, s32[16,32]{1,0:T(8,128)} %bitcast.4, s32[16,32]{1,0:T(8,128)} %bitcast.5, s32[1,32]{1,0:T(1,128)} %bitcast.6, f32[16,8,128]{2,1,0:T(8,128)} %rp_hbm.1, f32[16,8,128]{2,1,0:T(8,128)} %rd_hbm.1), custom_call_target="tpu_custom_call" | custom-call | tf_op jit(solution)/shard_map/pallas_call | solution.py:623
  20.8 1.0 %shard_map.78 = (f32[32,8,32]{2,1,0:T(8,128)}, f32[8,32]{1,0:T(8,128)}) custom-call(f32[4,9,8,128]{3,2,1,0:T(8,128)S(1)} %shard_map.77.home), custom_call_target="tpu_custom_call" | custom-call | tf_op jit(solution)/shard_map/pallas_call | solution.py:673

commit v5 on v4

--- a/solution.py
+++ b/solution.py
@@ -205,49 +205,52 @@
     def slot_copy(p, slot, to):
         return pltpu.make_async_remote_copy(
             src_ref=send.at[p, 0:5], dst_ref=recv.at[slot, 0:5],
-            send_sem=send_sem.at[lax.rem(to, 2), p], recv_sem=recv_sem.at[slot],
+            send_sem=send_sem.at[lax.rem(to, 2)], recv_sem=recv_sem.at[0],
             device_id=(p, to), device_id_type=MESH,
         )
+
+    def wait_all(ref, sem):
+        pltpu.make_async_copy(ref, ref, sem).wait()
 
     def data_copy(p, slot):
         return pltpu.make_async_remote_copy(
             src_ref=data, dst_ref=data_in.at[slot],
-            send_sem=data_send_sem.at[p], recv_sem=data_recv_sem.at[slot],
+            send_sem=data_send_sem.at[0], recv_sem=data_recv_sem.at[0],
             device_id=(q * rows + p, core), device_id_type=MESH,
         )
 
     def p_copy(p, slot):
         return pltpu.make_async_remote_copy(
             src_ref=out_p.at[p], dst_ref=in_p.at[slot],
-            send_sem=p_send_sem.at[p], recv_sem=p_recv_sem.at[slot],
+            send_sem=p_send_sem.at[0], recv_sem=p_recv_sem.at[0],
             device_id=(q * rows + p, core), device_id_type=MESH,
         )
 
     def w_copy(p, slot):
         return pltpu.make_async_remote_copy(
             src_ref=out_w.at[p], dst_ref=in_w.at[slot],
-            send_sem=w_send_sem.at[p], recv_sem=w_recv_sem.at[slot],
+            send_sem=w_send_sem.at[0], recv_sem=w_recv_sem.at[(p ^ z) - 1],
             device_id=(q * rows + p, core), device_id_type=MESH,
         )
 
     def root_data_copy(slot):
         return pltpu.make_async_remote_copy(
             src_ref=data, dst_ref=root_data.at[slot],
-            send_sem=root_send_sem.at[0], recv_sem=root_data_sem.at[slot],
+            send_sem=root_send_sem.at[0], recv_sem=root_data_sem.at[0],
             device_id=(0, core), device_id_type=MESH,
         )
 
     def root_copy(slot):
         return pltpu.make_async_remote_copy(
             src_ref=out_r, dst_ref=root_in.at[slot],
-            send_sem=root_send_sem.at[1], recv_sem=root_recv_sem.at[slot],
+            send_sem=root_send_sem.at[1], recv_sem=root_recv_sem.at[0],
             device_id=(0, core), device_id_type=MESH,
         )
 
     def back_copy(p, slot):
         return pltpu.make_async_remote_copy(
             src_ref=back.at[p], dst_ref=home.at[slot],
-            send_sem=back_send_sem.at[p], recv_sem=back_recv_sem.at[slot],
+            send_sem=back_send_sem.at[0], recv_sem=back_recv_sem.at[0],
             device_id=(p * rows + z, core), device_id_type=MESH,
         )
 
@@ -325,15 +328,13 @@
     observed = jnp.concatenate([obs[:, i, :] for i in range(8)], 0)
     observed = jnp.concatenate(split(observed, 3), 0)
 
-    @pl.loop(1, n)
-    def _(d):
-        p = me ^ d
-        slot_copy(p, p, pair).wait_recv()
-
-    @pl.when(jnp.logical_not(odd))
-    def _():
-        slot_copy(me, me, pair).wait_recv()
-
+    @pl.when(odd)
+    def _():
+        wait_all(recv.at[0 : n - 1, 0:5], recv_sem.at[0])
+
+    @pl.when(even)
+    def _():
+        wait_all(recv.at[:, 0:5], recv_sem.at[0])
 
     row32 = lax.broadcasted_iota(jnp.int32, (32, 128), 0)
     codes, matrices = [], []
@@ -467,9 +468,9 @@
     in_w[z] = out_w[z]
     for k in range(rows):
         p = z ^ k
-        if k > 0:
-            data_copy(p, p).wait_recv()
-            p_copy(p, p).wait_recv()
+        if k == 1:
+            wait_all(data_in.at[0 : rows - 1], data_recv_sem.at[0])
+            wait_all(in_p.at[0 : rows - 1], p_recv_sem.at[0])
         place = in_p[p]
         hot = jnp.where(row16 == jnp.concatenate([place, place], 0), 1.0, 0.0).astype(BF16)
         for i in range(8):
@@ -540,7 +541,8 @@
             hot = jnp.concatenate(
                 [jnp.where(row < 64, hot, 0.0), jnp.where(row < 64, 0.0, hot)], 1
             ).astype(BF16)
-            root_data_copy(p).wait_recv()
+            if p == 0:
+                wait_all(root_data, root_data_sem.at[0])
             left = jnp.concatenate(split(root_data[p].reshape(128, 128), 2), 1)
             both = dot(left, jnp.concatenate([hot, hot], 0))
             for m in range(2):
@@ -548,7 +550,8 @@
         sums = [None] * 32
         power = None
         for p in range(rows):
-            root_copy(p).wait_recv()
+            if p == 0:
+                wait_all(root_in, root_recv_sem.at[0])
             u, v, part = (root_in[p, 8 * m : 8 * m + 8] for m in range(3))
             power = part if p == 0 else power + part
             for s in range(16):
@@ -570,36 +573,31 @@
         home[3, 8] = gains
 
     home[q] = back[q]
-    for k in range(1, 4):
-        p = lax.rem(q + k, 4)
-
-        @pl.when(jnp.logical_not(jnp.logical_and(root, p == 3)))
-        def _():
-            back_copy(p, p).wait_recv()
+
+    @pl.when(jnp.logical_not(root))
+    def _():
+        wait_all(home.at[0:3], back_recv_sem.at[0])
+
+    @pl.when(root)
+    def _():
+        wait_all(home.at[0:2], back_recv_sem.at[0])
 
     @pl.when(odd)
     def _():
-        @pl.loop(1, n)
-        def _(k):
-            p = me ^ k
-            slot_copy(p, p, pair).wait_send()
-            slot_copy(p, p, core).wait_send()
-
-        slot_copy(me, me, pair).wait_send()
-
-    @pl.loop(1, rows)
-    def _(k):
-        p = lax.rem(z + k, rows)
-        data_copy(p, p).wait_send()
-        p_copy(p, p).wait_send()
-        w_copy(p, p).wait_send()
-
-    for k in range(1, 4):
-        p = lax.rem(q + k, 4)
-
-        @pl.when(jnp.logical_not(to_root(p)))
-        def _():
-            back_copy(p, p).wait_send()
+        wait_all(send.at[:, 0:5], send_sem.at[0])
+        wait_all(send.at[0 : n - 1, 0:5], send_sem.at[1])
+
+    wait_all(data_in.at[0 : rows - 1], data_send_sem.at[0])
+    wait_all(in_p.at[0 : rows - 1], p_send_sem.at[0])
+    wait_all(in_w.at[0 : rows - 1], w_send_sem.at[0])
+
+    @pl.when(to_root(0))
+    def _():
+        wait_all(back.at[0:2], back_send_sem.at[0])
+
+    @pl.when(jnp.logical_not(to_root(0)))
+    def _():
+        wait_all(back.at[0:3], back_send_sem.at[0])
 
     @pl.when(far)
     def _():
@@ -652,19 +650,19 @@
             pltpu.VMEM((24, 128), F32),
             pltpu.VMEM((rows, 24, 128), F32),
             pltpu.SemaphoreType.DMA((6,)),
-            pltpu.SemaphoreType.DMA((2, n)),
-            pltpu.SemaphoreType.DMA((n,)),
-            pltpu.SemaphoreType.DMA((rows,)),
-            pltpu.SemaphoreType.DMA((rows,)),
-            pltpu.SemaphoreType.DMA((rows,)),
-            pltpu.SemaphoreType.DMA((rows,)),
-            pltpu.SemaphoreType.DMA((rows,)),
-            pltpu.SemaphoreType.DMA((rows,)),
-            pltpu.SemaphoreType.DMA((4,)),
-            pltpu.SemaphoreType.DMA((4,)),
             pltpu.SemaphoreType.DMA((2,)),
-            pltpu.SemaphoreType.DMA((rows,)),
-            pltpu.SemaphoreType.DMA((rows,)),
+            pltpu.SemaphoreType.DMA((1,)),
+            pltpu.SemaphoreType.DMA((1,)),
+            pltpu.SemaphoreType.DMA((1,)),
+            pltpu.SemaphoreType.DMA((1,)),
+            pltpu.SemaphoreType.DMA((1,)),
+            pltpu.SemaphoreType.DMA((1,)),
+            pltpu.SemaphoreType.DMA((rows - 1,)),
+            pltpu.SemaphoreType.DMA((1,)),
+            pltpu.SemaphoreType.DMA((1,)),
+            pltpu.SemaphoreType.DMA((2,)),
+            pltpu.SemaphoreType.DMA((1,)),
+            pltpu.SemaphoreType.DMA((1,)),
         ],
         compiler_params=pltpu.CompilerParams(
             collective_id=0, has_side_effects=True, vmem_limit_bytes=65000 * 1024

time: 21.9 us -> 21.3 us (0.973)
  Pallas kernels: 21.1 us -> 20.5 us
    pallas_call x1, Pallas kernels: 20.2 us -> 19.5 us  [body(): pl.pallas_call(functools.partial(kernel, n), out_shape=pltpu.VMEM((4, 9,...]
where the time goes in v5:
time: 21.3 us; the launch traced here: 21.1 us
  Pallas kernels  20.5 us (96%)
  between operations  0.64 us (3%)
    pallas_call x1, Pallas kernels, body(): pl.pallas_call(functools.partial(kernel, n), out_shape=pltpu.VMEM((4, 9,...  19.5 us
    pallas_call x1, Pallas kernels, body(): pl.pallas_call(finish, out_shape=(jax.ShapeDtypeStruct((32, 8, 32), F32),...  0.96 us

profile of v5, /device:TPU:0, one launch (start us, length us, event | category | flops | bytes accessed | tf_op | source)
XLA Modules:
  0.0 21.1 jit_solution(4609356366241200722)
XLA Ops:
  0.6 19.5 %shard_map.77.home = f32[4,9,8,128]{3,2,1,0:T(8,128)S(1)} custom-call(f32[32,512]{1,0:T(8,128)} %cov_hbm.1, s32[16,32]{1,0:T(8,128)} %bitcast.4, s32[16,32]{1,0:T(8,128)} %bitcast.5, s32[1,32]{1,0:T(1,128)} %bitcast.6, f32[16,8,128]{2,1,0:T(8,128)} %rp_hbm.1, f32[16,8,128]{2,1,0:T(8,128)} %rd_hbm.1), custom_call_target="tpu_custom_call" | custom-call | tf_op jit(solution)/shard_map/pallas_call | solution.py:621
  20.2 1.0 %shard_map.78 = (f32[32,8,32]{2,1,0:T(8,128)}, f32[8,32]{1,0:T(8,128)}) custom-call(f32[4,9,8,128]{3,2,1,0:T(8,128)S(1)} %shard_map.77.home), custom_call_target="tpu_custom_call" | custom-call | tf_op jit(solution)/shard_map/pallas_call | solution.py:671

commit v6 on v5

--- a/solution.py
+++ b/solution.py
@@ -176,9 +176,7 @@
 
     @pl.when(jnp.logical_not(odd))
     def _():
-        @pl.loop(0, n)
-        def _(d):
-            greet(me ^ (n - 1 - d), pair)
+        greet(me, pair)
 
         @pl.loop(1, rows)
         def _(d):
@@ -284,11 +282,7 @@
             tiles = [jnp.where(row8 < 3, pltpu.roll(x, 7, 0), pltpu.roll(x, 5, 0)) for x in tiles]
             for j, tile in enumerate(lane_groups(tiles)):
                 send[4 * t + j] = tile
-        pl.semaphore_wait(barrier, 2 * n - 1)
-
-        @pl.loop(0, n)
-        def _(d):
-            slot_copy(me ^ (n - 1 - d), me, pair).start()
+        pl.semaphore_wait(barrier, n)
 
         @pl.loop(1, n)
         def _(d):
@@ -331,6 +325,11 @@
     @pl.when(odd)
     def _():
         wait_all(recv.at[0 : n - 1, 0:5], recv_sem.at[0])
+        pltpu.make_async_remote_copy(
+            src_ref=recv.at[:, 0:5], dst_ref=recv.at[:, 0:5],
+            send_sem=send_sem.at[0], recv_sem=recv_sem.at[0],
+            device_id=(me, pair), device_id_type=MESH,
+        ).start()
 
     @pl.when(even)
     def _():

time: 21.3 us -> 21.1 us (level)
  no operation moved by 1% of the time
where the time goes in v6:
time: 21.1 us; the launch traced here: 20.9 us
  Pallas kernels  20.3 us (96%)
  between operations  0.64 us (3%)
    pallas_call x1, Pallas kernels, body(): pl.pallas_call(functools.partial(kernel, n), out_shape=pltpu.VMEM((4, 9,...  19.3 us
    pallas_call x1, Pallas kernels, body(): pl.pallas_call(finish, out_shape=(jax.ShapeDtypeStruct((32, 8, 32), F32),...  0.96 us

profile of v6, /device:TPU:0, one launch (start us, length us, event | category | flops | bytes accessed | tf_op | source)
XLA Modules:
  0.0 20.9 jit_solution(14514687338319916006)
XLA Ops:
  0.6 19.3 %shard_map.77.home = f32[4,9,8,128]{3,2,1,0:T(8,128)S(1)} custom-call(f32[32,512]{1,0:T(8,128)} %cov_hbm.1, s32[16,32]{1,0:T(8,128)} %bitcast.4, s32[16,32]{1,0:T(8,128)} %bitcast.5, s32[1,32]{1,0:T(1,128)} %bitcast.6, f32[16,8,128]{2,1,0:T(8,128)} %rp_hbm.1, f32[16,8,128]{2,1,0:T(8,128)} %rd_hbm.1), custom_call_target="tpu_custom_call" | custom-call | tf_op jit(solution)/shard_map/pallas_call | solution.py:620
  20.0 1.0 %shard_map.78 = (f32[32,8,32]{2,1,0:T(8,128)}, f32[8,32]{1,0:T(8,128)}) custom-call(f32[4,9,8,128]{3,2,1,0:T(8,128)S(1)} %shard_map.77.home), custom_call_target="tpu_custom_call" | custom-call | tf_op jit(solution)/shard_map/pallas_call | solution.py:670

commit v7 on v6

--- a/solution.py
+++ b/solution.py
@@ -16,6 +16,7 @@
 REAL = dict(zip(PAIRS, [0, 1, 2, 3, 4, 10]))
 IMAG = dict(zip(PAIRS, [16, 17, 18, 19, 20, 26]))
 CODE = 24
+DIRECT = 2
 
 
 def split(x, parts):
@@ -154,12 +155,12 @@
         (cl_hbm, cl_ref), (valid_hbm, valid_ref), (pilot_hbm, pilot_ref),
         (cov_hbm, cov_ref), (rp_hbm, rp_ref), (rd_hbm, rd_ref),
     ]
-    loads = [pltpu.make_async_copy(a, b, load_sem.at[i]) for i, (a, b) in enumerate(pairs)]
+    loads = [pltpu.make_async_copy(a, b, load_sem.at[min(i, 4)]) for i, (a, b) in enumerate(pairs)]
     odd = lax.rem(core, 2) == 1
     pair = core ^ 1
     even = jnp.logical_not(odd)
     root = jnp.logical_and(me == 0, even)
-    far = jnp.logical_and(q == 3, even)
+    far = jnp.logical_and(q >= DIRECT, even)
     barrier = pltpu.get_barrier_semaphore()
 
     def greet(p, c):
@@ -190,9 +191,10 @@
         for load in loads[:2]:
             load.start()
 
-        @pl.loop(1, rows)
-        def _(c):
-            greet(3 * rows + c, core)
+        for d in range(DIRECT, 4):
+            @pl.loop(1, rows)
+            def _(c):
+                greet(d * rows + c, core)
 
     for load in loads[4:]:
         load.start()
@@ -300,8 +302,7 @@
     def _():
         pl.semaphore_wait(barrier, rows + 2)
 
-    for load in loads[4:]:
-        load.wait()
+    wait_all(data_in.at[0:2], load_sem.at[4])
     turned = jnp.concatenate([rd_ref[:, f, :] for f in range(8)], 0).T.reshape(16, 8, 128)
     for f, tile in enumerate(block_transpose([turned[:, i, :] for i in range(8)])):
         data[:, f, :] = tile
@@ -312,7 +313,7 @@
 
     @pl.when(far)
     def _():
-        root_data_copy(z).start()
+        root_data_copy(me - DIRECT * rows).start()
 
     turned = jnp.concatenate([rp_ref[:, f, :] for f in range(8)], 0).T
     for half in range(2):
@@ -456,7 +457,7 @@
                         packed = jnp.where(quarter == j, pltpu.roll(out_w[0, at : at + 8], 32 * j, 1), packed)
                     out_r[8 * m : 8 * m + 8] = packed
                 out_r[16:24] = out_w[0, 64:72]
-                root_copy(z).start()
+                root_copy(me - DIRECT * rows).start()
 
         @pl.when(z != g)
         def _():
@@ -534,8 +535,8 @@
         row = lax.broadcasted_iota(jnp.int32, (128, 128), 0)
         quarter = lax.broadcasted_iota(jnp.int32, (128, 128), 1) // 32
         base = jnp.where(((row >> 4) & 3) == quarter, ((row & 15) + 1).astype(F32), -1.0)
-        for p in range(rows):
-            place = jnp.sum(jnp.where(owner == 3 * rows + p, mark, 0.0), 0, keepdims=True)
+        for p in range((4 - DIRECT) * rows):
+            place = jnp.sum(jnp.where(owner == DIRECT * rows + p, mark, 0.0), 0, keepdims=True)
             hot = jnp.where(base == place, 1.0, 0.0)
             hot = jnp.concatenate(
                 [jnp.where(row < 64, hot, 0.0), jnp.where(row < 64, 0.0, hot)], 1
@@ -548,7 +549,7 @@
                 root_held[p, m] = both[:, 128 * m : 128 * m + 128].reshape(16, 8, 128)
         sums = [None] * 32
         power = None
-        for p in range(rows):
+        for p in range((4 - DIRECT) * rows):
             if p == 0:
                 wait_all(root_in, root_recv_sem.at[0])
             u, v, part = (root_in[p, 8 * m : 8 * m + 8] for m in range(3))
@@ -570,6 +571,8 @@
         for j in range(1, 4):
             gains = gains + pltpu.roll(turned[8 * j : 8 * j + 8], 8 * j, 1)
         home[3, 8] = gains
+        for p in range(DIRECT, 3):
+            home[p] = jnp.zeros_like(home[p])
 
     home[q] = back[q]
 
@@ -579,7 +582,7 @@
 
     @pl.when(root)
     def _():
-        wait_all(home.at[0:2], back_recv_sem.at[0])
+        wait_all(home.at[0 : DIRECT - 1], back_recv_sem.at[0])
 
     @pl.when(odd)
     def _():
@@ -600,8 +603,8 @@
 
     @pl.when(far)
     def _():
-        root_data_copy(z).wait_send()
-        root_copy(z).wait_send()
+        root_data_copy(me - DIRECT * rows).wait_send()
+        root_copy(me - DIRECT * rows).wait_send()
 
 
 def finish(home, sym_ref, gain_ref):
@@ -644,11 +647,11 @@
             pltpu.VMEM((rows, 72, 128), F32),
             pltpu.VMEM((rows, 72, 128), F32),
             pltpu.VMEM((4, 9, 8, 128), F32),
-            pltpu.VMEM((rows, 16, 8, 128), F32),
-            pltpu.VMEM((rows, 2, 16, 8, 128), F32),
+            pltpu.VMEM(((4 - DIRECT) * rows, 16, 8, 128), F32),
+            pltpu.VMEM(((4 - DIRECT) * rows, 2, 16, 8, 128), F32),
             pltpu.VMEM((24, 128), F32),
-            pltpu.VMEM((rows, 24, 128), F32),
-            pltpu.SemaphoreType.DMA((6,)),
+            pltpu.VMEM(((4 - DIRECT) * rows, 24, 128), F32),
+            pltpu.SemaphoreType.DMA((5,)),
             pltpu.SemaphoreType.DMA((2,)),
             pltpu.SemaphoreType.DMA((1,)),
             pltpu.SemaphoreType.DMA((1,)),

time: 21.1 us -> 21 us (level)
  no operation moved by 1% of the time
where the time goes in v7:
time: 21 us; the launch traced here: 20.9 us
  Pallas kernels  20.2 us (96%)
  between operations  0.64 us (3%)
    pallas_call x1, Pallas kernels, body(): pl.pallas_call(functools.partial(kernel, n), out_shape=pltpu.VMEM((4, 9,...  19.3 us
    pallas_call x1, Pallas kernels, body(): pl.pallas_call(finish, out_shape=(jax.ShapeDtypeStruct((32, 8, 32), F32),...  0.96 us

profile of v7, /device:TPU:0, one launch (start us, length us, event | category | flops | bytes accessed | tf_op | source)
XLA Modules:
  0.0 20.9 jit_solution(8014048320026161737)
XLA Ops:
  0.6 19.3 %shard_map.77.home = f32[4,9,8,128]{3,2,1,0:T(8,128)S(1)} custom-call(f32[32,512]{1,0:T(8,128)} %cov_hbm.1, s32[16,32]{1,0:T(8,128)} %bitcast.4, s32[16,32]{1,0:T(8,128)} %bitcast.5, s32[1,32]{1,0:T(1,128)} %bitcast.6, f32[16,8,128]{2,1,0:T(8,128)} %rp_hbm.1, f32[16,8,128]{2,1,0:T(8,128)} %rd_hbm.1), custom_call_target="tpu_custom_call" | custom-call | tf_op jit(solution)/shard_map/pallas_call | solution.py:623
  19.9 1.0 %shard_map.78 = (f32[32,8,32]{2,1,0:T(8,128)}, f32[8,32]{1,0:T(8,128)}) custom-call(f32[4,9,8,128]{3,2,1,0:T(8,128)S(1)} %shard_map.77.home), custom_call_target="tpu_custom_call" | custom-call | tf_op jit(solution)/shard_map/pallas_call | solution.py:673

commit v8 on v6

--- a/solution.py
+++ b/solution.py
@@ -154,7 +154,7 @@
         (cl_hbm, cl_ref), (valid_hbm, valid_ref), (pilot_hbm, pilot_ref),
         (cov_hbm, cov_ref), (rp_hbm, rp_ref), (rd_hbm, rd_ref),
     ]
-    loads = [pltpu.make_async_copy(a, b, load_sem.at[i]) for i, (a, b) in enumerate(pairs)]
+    loads = [pltpu.make_async_copy(a, b, load_sem.at[min(i, 4)]) for i, (a, b) in enumerate(pairs)]
     odd = lax.rem(core, 2) == 1
     pair = core ^ 1
     even = jnp.logical_not(odd)
@@ -227,7 +227,7 @@
     def w_copy(p, slot):
         return pltpu.make_async_remote_copy(
             src_ref=out_w.at[p], dst_ref=in_w.at[slot],
-            send_sem=w_send_sem.at[0], recv_sem=w_recv_sem.at[(p ^ z) - 1],
+            send_sem=w_send_sem.at[0], recv_sem=w_recv_sem.at[0],
             device_id=(q * rows + p, core), device_id_type=MESH,
         )
 
@@ -300,8 +300,7 @@
     def _():
         pl.semaphore_wait(barrier, rows + 2)
 
-    for load in loads[4:]:
-        load.wait()
+    wait_all(data_in.at[0:2], load_sem.at[4])
     turned = jnp.concatenate([rd_ref[:, f, :] for f in range(8)], 0).T.reshape(16, 8, 128)
     for f, tile in enumerate(block_transpose([turned[:, i, :] for i in range(8)])):
         data[:, f, :] = tile
@@ -488,8 +487,8 @@
     power = None
     for k in range(rows):
         p = z ^ k
-        if k > 0:
-            w_copy(p, p).wait_recv()
+        if k == 1:
+            wait_all(in_w.at[0 : rows - 1], w_recv_sem.at[0])
         u = [in_w[p, 8 * i : 8 * i + 8] for i in range(8)]
         part = in_w[p, 64:72]
         power = part if power is None else power + part
@@ -648,7 +647,7 @@
             pltpu.VMEM((rows, 2, 16, 8, 128), F32),
             pltpu.VMEM((24, 128), F32),
             pltpu.VMEM((rows, 24, 128), F32),
-            pltpu.SemaphoreType.DMA((6,)),
+            pltpu.SemaphoreType.DMA((5,)),
             pltpu.SemaphoreType.DMA((2,)),
             pltpu.SemaphoreType.DMA((1,)),
             pltpu.SemaphoreType.DMA((1,)),
@@ -656,7 +655,7 @@
             pltpu.SemaphoreType.DMA((1,)),
             pltpu.SemaphoreType.DMA((1,)),
             pltpu.SemaphoreType.DMA((1,)),
-            pltpu.SemaphoreType.DMA((rows - 1,)),
+            pltpu.SemaphoreType.DMA((1,)),
             pltpu.SemaphoreType.DMA((1,)),
             pltpu.SemaphoreType.DMA((1,)),
             pltpu.SemaphoreType.DMA((2,)),

time: 21.1 us -> 21.2 us (level)
  no operation moved by 1% of the time
where the time goes in v8:
time: 21.2 us; the launch traced here: 21 us
  Pallas kernels  20.4 us (96%)
  between operations  0.64 us (3%)
    pallas_call x1, Pallas kernels, body(): pl.pallas_call(functools.partial(kernel, n), out_shape=pltpu.VMEM((4, 9,...  19.4 us
    pallas_call x1, Pallas kernels, body(): pl.pallas_call(finish, out_shape=(jax.ShapeDtypeStruct((32, 8, 32), F32),...  0.96 us

profile of v8, /device:TPU:0, one launch (start us, length us, event | category | flops | bytes accessed | tf_op | source)
XLA Modules:
  0.0 21.0 jit_solution(7111869547696263906)
XLA Ops:
  0.6 19.4 %shard_map.77.home = f32[4,9,8,128]{3,2,1,0:T(8,128)S(1)} custom-call(f32[32,512]{1,0:T(8,128)} %cov_hbm.1, s32[16,32]{1,0:T(8,128)} %bitcast.4, s32[16,32]{1,0:T(8,128)} %bitcast.5, s32[1,32]{1,0:T(1,128)} %bitcast.6, f32[16,8,128]{2,1,0:T(8,128)} %rp_hbm.1, f32[16,8,128]{2,1,0:T(8,128)} %rd_hbm.1), custom_call_target="tpu_custom_call" | custom-call | tf_op jit(solution)/shard_map/pallas_call | solution.py:619
  20.1 1.0 %shard_map.78 = (f32[32,8,32]{2,1,0:T(8,128)}, f32[8,32]{1,0:T(8,128)}) custom-call(f32[4,9,8,128]{3,2,1,0:T(8,128)S(1)} %shard_map.77.home), custom_call_target="tpu_custom_call" | custom-call | tf_op jit(solution)/shard_map/pallas_call | solution.py:669
